TPU v7x, 32 devices: a whole 2x2x4 slice. The times are simulated.
32 devices in a mesh: dp: 8 (over z, x), tensor: 4 (over y, core).
Axes of the slice: x: 2, y: 2, z: 4, core: 2. Of those that a mesh axis runs over, the one named last changes fastest.
Arguments:
- block_input: bfloat16 [8192, 1152], P('dp'), may hold values from -24 to 24
- conditions: float32 [32, 1152], replicated, may hold values from -6 to 6
- segment_ids: int32 [8, 1024], P('dp'), may hold values from 0 to 7, never falling along the last dimension, each value on 1 to 256 neighbouring positions
- segment_cond: int32 [8, 8], P('dp'), may hold values from 0 to 31
- cotangent: bfloat16 [8192, 1152], P('dp'), may hold values from -6 to 6
- qkv_weight: float32 [1152, 3, 1152], P('dp', None, 'tensor'), may hold values from -0.1875 to 0.1875
- proj_weight: float32 [1152, 1152], P(('tensor', 'dp')), may hold values from -1.5 to 1.5
- inner_weight: float32 [1152, 4608], P('dp', 'tensor'), may hold values from -0.1875 to 0.1875
- outer_weight: float32 [4608, 1152], P(('tensor', 'dp')), may hold values from -0.1875 to 0.1875
- ada_weight: float32 [6, 1152, 1152], P(None, 'tensor'), may hold values from -0.1875 to 0.1875
- head_biases: float32 [9, 1152], P(None, 'tensor'), may hold values from -1.8 to 1.8
- inner_bias: float32 [4608], P('tensor'), may hold values from -1.8 to 1.8
- shared_biases: float32 [2, 1152], replicated, may hold values from -1.8 to 1.8
- qkv_first: float32 [1152, 3, 1152], P('dp', None, 'tensor'), may hold values from -160 to 160
- proj_first: float32 [1152, 1152], P(('tensor', 'dp')), may hold values from -32 to 32
- inner_first: float32 [1152, 4608], P('dp', 'tensor'), may hold values from -256 to 256
- outer_first: float32 [4608, 1152], P(('tensor', 'dp')), may hold values from -192 to 192
- ada_first: float32 [6, 1152, 1152], P(None, 'tensor'), may hold values from -320 to 320
- head_biases_first: float32 [9, 1152], P(None, 'tensor'), may hold values from -384 to 384
- inner_bias_first: float32 [4608], P('tensor'), may hold values from -256 to 256
- shared_biases_first: float32 [2, 1152], replicated, may hold values from -384 to 384
- qkv_second: float32 [1152, 3, 1152], P('dp', None, 'tensor'), may hold values from 522.88 to 2092.8
- proj_second: float32 [1152, 1152], P(('tensor', 'dp')), may hold values from 20.928 to 83.648
- inner_second: float32 [1152, 4608], P('dp', 'tensor'), may hold values from 1105.92 to 4423.68
- outer_second: float32 [4608, 1152], P(('tensor', 'dp')), may hold values from 707.7888 to 2831.1553
- ada_second: float32 [6, 1152, 1152], P(None, 'tensor'), may hold values from 1966.08 to 7864.32
- head_biases_second: float32 [9, 1152], P(None, 'tensor'), may hold values from 2678.784 to 10706.944
- inner_bias_second: float32 [4608], P('tensor'), may hold values from 1105.92 to 4423.68
- shared_biases_second: float32 [2, 1152], replicated, may hold values from 2678.784 to 10706.944
Outputs:
- block_output: bfloat16 [8192, 1152], P(('dp', 'tensor'))
- input_grad: float32 [8192, 1152], P(('dp', 'tensor'))
- cond_grad: float32 [32, 1152], replicated
- qkv_updated: float32 [1152, 3, 1152], P('dp', None, 'tensor')
- proj_updated: float32 [1152, 1152], P(('tensor', 'dp'))
- inner_updated: float32 [1152, 4608], P('dp', 'tensor')
- outer_updated: float32 [4608, 1152], P(('tensor', 'dp'))
- ada_updated: float32 [6, 1152, 1152], P(None, 'tensor')
- head_biases_updated: float32 [9, 1152], P(None, 'tensor')
- inner_bias_updated: float32 [4608], P('tensor')
- shared_biases_updated: float32 [2, 1152], replicated
- qkv_first_new: float32 [1152, 3, 1152], P('dp', None, 'tensor')
- proj_first_new: float32 [1152, 1152], P(('tensor', 'dp'))
- inner_first_new: float32 [1152, 4608], P('dp', 'tensor')
- outer_first_new: float32 [4608, 1152], P(('tensor', 'dp'))
- ada_first_new: float32 [6, 1152, 1152], P(None, 'tensor')
- head_biases_first_new: float32 [9, 1152], P(None, 'tensor')
- inner_bias_first_new: float32 [4608], P('tensor')
- shared_biases_first_new: float32 [2, 1152], replicated
- qkv_second_new: float32 [1152, 3, 1152], P('dp', None, 'tensor')
- proj_second_new: float32 [1152, 1152], P(('tensor', 'dp'))
- inner_second_new: float32 [1152, 4608], P('dp', 'tensor')
- outer_second_new: float32 [4608, 1152], P(('tensor', 'dp'))
- ada_second_new: float32 [6, 1152, 1152], P(None, 'tensor')
- head_biases_second_new: float32 [9, 1152], P(None, 'tensor')
- inner_bias_second_new: float32 [4608], P('tensor')
- shared_biases_second_new: float32 [2, 1152], replicated
- qkv_copy: bfloat16 [1152, 3, 1152], P('dp', None, 'tensor')
- projection_bfloat_copy: bfloat16 [1152, 1152], P(('tensor', 'dp'))
- inner_copy: bfloat16 [1152, 4608], P('dp', 'tensor')
- outer_copy: bfloat16 [4608, 1152], P(('tensor', 'dp'))
Inputs may be any that keep to these rules, and one draw needn't show every extreme that they name: `segment_ids`: in each row segment numbers start at 0 and never fall; each of the 8 images holds at most 256 positions.
All inputs are finite; a program needn't handle non-finite values.
Results may differ from a plain program's by a relative error of at most 0.018.
The roundings to bfloat16 on the way count: a program that leaves them out, or rounds other values in their place, can miss the bound.
Values may be sent and summed in bfloat16 or wider, within the bound.
A program may use at most 256 MiB of HBM per device.

v0:
```python
import functools
import math

import jax
import jax.numpy as jnp
import numpy as np
from jax import lax
from jax.experimental import pallas as pl
from jax.experimental.pallas import tpu as pltpu
from jax.sharding import PartitionSpec as P

HD = 72
STEP = 10


BETA_ONE = 0.5
BETA_TWO = 0.6
ADAM_EPS = 1e-08
DECAY = 0.01
NORM_EPSILON = 1e-06
RATES = (0.04, 0.3, 0.04, 0.04, 0.04, 0.4, 0.4, 0.4)
PRECISION_MAX = lax.Precision.HIGHEST
FLOAT = jnp.float32
HALF = jnp.bfloat16
DP, TP = "dp", "tensor"


def silu(values):
    return values / (1.0 + jnp.exp(-values))


def gelu_tanh(values):
    inner = math.sqrt(2.0 / math.pi) * (values + 0.044715 * values * values * values)
    return 0.5 * values * (1.0 + jnp.tanh(inner))


def normalize(values):
    centered = values - jnp.mean(values, axis=-1, keepdims=True)
    inv_std = lax.rsqrt(jnp.mean(centered * centered, axis=-1, keepdims=True) + NORM_EPSILON)
    return (centered * inv_std, inv_std)


def norm_back(grad_normed, normed, inv_std):
    first_mean = jnp.mean(grad_normed, axis=-1, keepdims=True)
    second_mean = jnp.mean(grad_normed * normed, axis=-1, keepdims=True)
    return inv_std * (grad_normed - first_mean - normed * second_mean)


def block_scores(query_block, keys, query_segs, key_segs):
    scores = jnp.einsum("qhe,khe->hqk", query_block, keys, preferred_element_type=FLOAT) * (
        1.0 / math.sqrt(HD)
    )
    same = query_segs[:, None] == key_segs[None, :]
    return jnp.where(same[None], scores, -1e30)


def attend_forward(row_qkv, row_segs):
    queries = row_qkv[:, 0]
    keys = row_qkv[:, 1]
    values = row_qkv[:, 2]
    length = queries.shape[0]
    heads_local = queries.shape[1]
    block = min(512, length)
    blocks = length // block

    def one_block(pieces):
        query_block, query_segs = pieces
        scores = block_scores(query_block, keys, query_segs, row_segs)
        top = jnp.max(scores, axis=-1, keepdims=True)
        expo = jnp.exp(scores - top)
        total = jnp.sum(expo, axis=-1, keepdims=True)
        probs = (expo / total).astype(HALF)
        attended = jnp.einsum("hqk,khe->qhe", probs, values, preferred_element_type=FLOAT)
        return (attended, (top + jnp.log(total))[:, :, 0])

    attended, log_totals = lax.map(
        one_block,
        (queries.reshape(blocks, block, heads_local, HD), row_segs.reshape(blocks, block)),
    )
    return (attended.reshape(length, heads_local, HD), log_totals)


def attend_backward(row_qkv, row_segs, grad_row, log_totals):
    queries = row_qkv[:, 0]
    keys = row_qkv[:, 1]
    values = row_qkv[:, 2]
    length = queries.shape[0]
    heads_local = queries.shape[1]
    block = min(512, length)
    blocks = length // block
    scale = 1.0 / math.sqrt(HD)

    def one_block(carry, pieces):
        key_sum, value_sum = carry
        query_block, query_segs, grad_block, block_total = pieces
        scores = block_scores(query_block, keys, query_segs, row_segs)
        probs = jnp.exp(scores - block_total[:, :, None])
        grad_probs = jnp.einsum("qhe,khe->hqk", grad_block, values, preferred_element_type=FLOAT)
        center = jnp.sum(probs * grad_probs, axis=-1, keepdims=True)
        grad_scores = (probs * (grad_probs - center)).astype(HALF)
        grad_query = (
            jnp.einsum("hqk,khe->qhe", grad_scores, keys, preferred_element_type=FLOAT) * scale
        )
        key_sum = (
            key_sum
            + jnp.einsum("hqk,qhe->khe", grad_scores, query_block, preferred_element_type=FLOAT)
            * scale
        )
        value_sum = value_sum + jnp.einsum(
            "hqk,qhe->khe", probs.astype(HALF), grad_block, preferred_element_type=FLOAT
        )
        return ((key_sum, value_sum), grad_query)

    zeros = jnp.zeros((length, heads_local, HD), FLOAT)
    sums, grad_queries = lax.scan(
        one_block,
        (zeros, zeros),
        (
            queries.reshape(blocks, block, heads_local, HD),
            row_segs.reshape(blocks, block),
            grad_row.reshape(blocks, block, heads_local, HD),
            log_totals,
        ),
    )
    return jnp.stack([grad_queries.reshape(length, heads_local, HD), sums[0], sums[1]], axis=1)


def adam_update(weight, grad, first, second, rate):
    first_new = BETA_ONE * first + (1.0 - BETA_ONE) * grad
    second_new = BETA_TWO * second + (1.0 - BETA_TWO) * grad * grad
    fix_one = 1.0 - BETA_ONE**STEP
    fix_two = 1.0 - BETA_TWO**STEP
    update = first_new / fix_one / (jnp.sqrt(second_new / fix_two) + ADAM_EPS)
    return (weight - rate * (update + DECAY * weight), first_new, second_new)


def sum_to_shares(partial):
    return lax.psum_scatter(
        partial.astype(HALF), TP, scatter_dimension=0, tiled=True
    ).astype(FLOAT)


def sum_to_owners(partial):
    return lax.psum_scatter(
        partial.astype(HALF), DP, scatter_dimension=0, tiled=True
    ).astype(FLOAT)


SEG_MOST = 256
CORES = 2
MESH = pl.DeviceIdType.MESH
NT_DIMS = (((1,), (1,)), ((), ()))
TN_DIMS = (((0,), (0,)), ((), ()))
VMEM_BYTES = 62 * 1024 * 1024


def line_length(count):
    length = 1
    while (2 * length) ** 2 <= count:
        length *= 2
    return length


def mm(left, right):
    return jnp.dot(left, right, preferred_element_type=FLOAT)


def mm_nt(left, right):
    return lax.dot_general(left, right, NT_DIMS, preferred_element_type=FLOAT)


def mm_tn(left, right):
    return lax.dot_general(left, right, TN_DIMS, preferred_element_type=FLOAT)


def split_two(values):
    high = values.astype(HALF)
    return high, (values - high.astype(FLOAT)).astype(HALF)


def cond_picks(seg_cond, conds):
    return (lax.broadcasted_iota(jnp.int32, (conds, 1), 0) == seg_cond[...]).astype(FLOAT).astype(HALF)


def pick_rows(picks, values):
    high, rest = split_two(values)
    middle, low = split_two(values - high.astype(FLOAT))
    return mm_tn(picks, high) + mm_tn(picks, middle) + mm_tn(picks, low)


class Place:
    def __init__(self, dp_count, tensor_count):
        self.dp_count, self.tensor_count = dp_count, tensor_count
        self.xs = line_length(dp_count)
        self.zs = dp_count // self.xs
        self.ys = tensor_count // CORES
        self.dp, self.tensor = lax.axis_index(DP), lax.axis_index(TP)
        self.z, self.x = lax.div(self.dp, self.xs), lax.rem(self.dp, self.xs)
        self.y, self.core = lax.div(self.tensor, CORES), lax.rem(self.tensor, CORES)

    def z_of(self, step):
        return lax.rem(self.z + step + self.zs, self.zs)

    def x_of(self, step):
        return lax.rem(self.x + step + self.xs, self.xs)

    def z_peer(self, step):
        return (self.z_of(step) * self.xs + self.x, self.tensor)

    def x_peer(self, step):
        return (self.z * self.xs + self.x_of(step), self.tensor)

    def tensor_peer(self, step):
        return (self.dp, lax.rem(self.tensor + step, self.tensor_count))

    def core_peer(self):
        return (self.dp, self.y * CORES + 1 - self.core)

    def y_peer(self):
        return (self.dp, (1 - self.y) * CORES + self.core)

    def share_of(self, other_y, other_core):
        y = 1 - self.y if other_y else self.y
        core = 1 - self.core if other_core else self.core
        return y * CORES + core


def greet(peers):
    barrier = pltpu.get_barrier_semaphore()
    for peer in peers:
        pl.semaphore_signal(barrier, inc=1, device_id=peer, device_id_type=MESH)
    pl.semaphore_wait(barrier, len(peers))


def remote(src, dst, sends, recvs, peer):
    return pltpu.make_async_remote_copy(
        src_ref=src, dst_ref=dst, send_sem=sends, recv_sem=recvs, device_id=peer, device_id_type=MESH
    )


def rows_at(start, count):
    return pl.ds(pl.multiple_of(start, 16), count)


def unit_rows(shard):
    return 48 if shard % 48 == 0 else shard


class Gather:
    def __init__(self, place, pieces, z_sems, x_sems):
        self.place, self.pieces = place, pieces
        self.z_send, self.z_recv = z_sems
        self.x_send, self.x_recv = x_sems
        self.hops = place.zs - 1
        self.ticks = 0

    def slot(self, piece, z, x):
        full, shard, first, count = self.pieces[piece]
        return full.at[rows_at((z * self.place.xs + x) * shard + first, count)]

    def hop(self, piece, source, step, sem):
        at = self.place
        chunk = self.slot(piece, source, at.x)
        return remote(chunk, chunk, self.z_send.at[piece, sem], self.z_recv.at[piece, sem], at.z_peer(step))

    def x_copy(self, piece, source, step):
        at = self.place
        chunk = self.slot(piece, source, at.x)
        sems = self.x_send.at[piece, source, step - 1], self.x_recv.at[piece, source, step - 1]
        return remote(chunk, chunk, *sems, at.x_peer(step))

    def x_landing(self, piece, source, step):
        at = self.place
        chunk = self.slot(piece, source, at.x_of(-step))
        sems = self.x_send.at[piece, source, step - 1], self.x_recv.at[piece, source, step - 1]
        return remote(chunk, chunk, *sems, at.x_peer(step))

    def along_x(self, piece, source):
        for step in range(1, self.place.xs):
            self.x_copy(piece, source, step).start()

    def start(self, piece):
        at = self.place

        @pl.when(at.z < at.zs - 1)
        def _():
            self.hop(piece, at.z, 1, 0).start()

        @pl.when(at.z > 0)
        def _():
            self.hop(piece, at.z, -1, self.hops).start()

        self.along_x(piece, at.z)

    def pass_on(self, piece, away):
        at, hops = self.place, self.hops

        @pl.when(at.z >= away)
        def _():
            self.hop(piece, at.z - away, 1, away - 1).wait_recv()
            if away < hops:
                @pl.when(at.z < at.zs - 1)
                def _():
                    self.hop(piece, at.z - away, 1, away).start()
            self.along_x(piece, at.z - away)

        @pl.when(at.z + away < at.zs)
        def _():
            self.hop(piece, at.z + away, -1, hops + away - 1).wait_recv()
            if away < hops:
                @pl.when(at.z > 0)
                def _():
                    self.hop(piece, at.z + away, -1, hops + away).start()
            self.along_x(piece, at.z + away)

    def tick(self):
        now = self.ticks
        for away in range(1, self.hops + 1):
            if 0 <= now - away + 1 < len(self.pieces):
                self.pass_on(now - away + 1, away)
        if now + 3 < len(self.pieces):
            self.start(now + 3)
        self.ticks += 1

    def tick_until(self, piece):
        while self.ticks < min(piece, len(self.pieces) - 1) + self.hops:
            self.tick()

    def arrive(self, piece):
        at = self.place
        for source in range(at.zs):
            for step in range(1, at.xs):
                self.x_landing(piece, source, step).wait_recv()

    def finish(self, piece):
        at, hops = self.place, self.hops
        for away in range(hops):
            @pl.when((at.z >= away) & (at.z < at.zs - 1))
            def _(away=away):
                self.hop(piece, at.z - away, 1, away).wait_send()

            @pl.when((at.z + away < at.zs) & (at.z > 0))
            def _(away=away):
                self.hop(piece, at.z + away, -1, hops + away).wait_send()
        for source in range(at.zs):
            for step in range(1, at.xs):
                self.x_copy(piece, source, step).wait_send()


def layer_norm(values):
    mean = jnp.mean(values, axis=-1, keepdims=True)
    centered = values - mean
    inv_std = lax.rsqrt(jnp.mean(centered * centered, axis=-1, keepdims=True) + NORM_EPSILON)
    return centered * inv_std, inv_std


def forward_kernel(
    sizes,
    x_ref, seg_col, seg_row, seg_cond, cond_ref, ada_ref, head_bias, inner_bias, shared_bias,
    proj_place, wq_raw, wp_raw, wi_raw, wo_raw,
    wq_out, wp_out, wi_out, wo_out, hid_a_out, heads_out, lse_out, att_out, hid_b_out, act_out,
    slope_out, far_out, own_out, branch_out, middle_out, modk_out,
    wq_full, wp_full, wp_tight, wi_full, wo_full, hid_a, heads, lse, lse_heads, att_heads, att, part, core_in,
    y_out, y_in, hid_b, act, slope, ff_part, ff_in, ff_far, ff_own, branch, middle, modk, mods, ada_tile,
    wp_wide,
    z_send, z_recv, x_send, x_recv, mod_send, mod_recv, sum_send, sum_recv, gat_send, gat_recv, ff_send, ff_recv,
    ada_sem, save_sem,
):
    at = Place(sizes[DP], sizes[TP])
    tokens, width, columns, share = sizes["tokens"], sizes["width"], sizes["columns"], sizes["share"]
    nheads, segs = columns // HD, seg_cond.shape[1]
    window = min(tokens, share + 2 * SEG_MOST)
    greet(
        [at.z_peer(s) for s in range(1, at.zs)]
        + [at.x_peer(s) for s in range(1, at.xs)]
        + [at.tensor_peer(s) for s in range(1, at.tensor_count)]
    )
    pieces, lists = [], []
    for full, shard in (
        (wq_full, wq_raw.shape[1]), (wp_full, wp_wide.shape[0]), (wi_full, wi_raw.shape[0]), (wo_full, wo_raw.shape[0])
    ):
        unit = unit_rows(shard)
        lists.append(list(range(len(pieces), len(pieces) + shard // unit)))
        pieces += [(full, shard, first, unit) for first in range(0, shard, unit)]
    list_q, list_p, list_i, list_o = lists
    gather = Gather(at, pieces, (z_send, z_recv), (x_send, x_recv))
    last = len(pieces)

    def own_rows_of(full, shard):
        return rows_at(at.dp * shard, shard)

    wq_full[own_rows_of(wq_full, wq_raw.shape[1]), :] = jnp.concatenate(
        [wq_raw[part_index] for part_index in range(3)], axis=1
    ).astype(HALF)
    for piece in list_q[:3]:
        gather.start(piece)
    wp_wide[...] = jnp.zeros_like(wp_wide)
    wp_wide[0:wp_raw.shape[0], :] = wp_raw[...]
    for raw, full in ((wp_wide, wp_full), (wi_raw, wi_full), (wo_raw, wo_full)):
        full[own_rows_of(full, raw.shape[0]), :] = raw[...].astype(HALF)
    for piece in range(len(list_q[:3]), 3):
        gather.start(piece)

    def ada_copy(group):
        return pltpu.make_async_copy(ada_ref.at[group], ada_tile.at[group % 2], ada_sem.at[group % 2])

    ada_copy(0).start()
    cond_high, cond_low = split_two(silu(pick_rows(cond_picks(seg_cond, cond_ref.shape[0]), cond_ref[...])))
    cond_both = jnp.concatenate([cond_high, cond_low], axis=0)
    for group in range(6):
        if group == 3:
            gather.tick()
        if group < 5:
            ada_copy(group + 1).start()
        ada_copy(group).wait()
        weight_high, weight_low = split_two(ada_tile[group % 2])
        both = mm_nt(cond_both, weight_high)
        mods[at.tensor, group] = (
            both[:segs] + both[segs:] + mm_nt(cond_high, weight_low)
            + head_bias[3 + group:4 + group, :]
        )

    def mod_copy(step):
        own = mods.at[at.tensor]
        return remote(own, own, mod_send.at[step - 1], mod_recv.at[step - 1], at.tensor_peer(step))

    def mod_landing(step):
        landed = mods.at[lax.rem(at.tensor + at.tensor_count - step, at.tensor_count)]
        return remote(landed, landed, mod_send.at[step - 1], mod_recv.at[step - 1], at.tensor_peer(step))

    for step in range(1, at.tensor_count):
        mod_copy(step).start()
    gather.tick()
    for step in range(1, at.tensor_count):
        mod_landing(step).wait_recv()
    for group in range(6):
        whole = jnp.concatenate([mods[t, group] for t in range(at.tensor_count)], axis=1)
        high, low = split_two(whole)
        modk[group] = jnp.concatenate([high, low], axis=0)

    def pick(rows):
        ids = seg_col[rows, :]
        lanes = lax.broadcasted_iota(jnp.int32, (1, 2 * segs), 1)
        return (ids == lax.rem(lanes, segs)).astype(FLOAT).astype(HALF)

    gather.tick()

    def hidden_block(index, carry):
        rows = rows_at(index * share, share)
        normed, _ = layer_norm(x_ref[rows, :].astype(FLOAT))
        chosen = pick(rows)
        hid_a[rows, :] = (normed * (1.0 + mm(chosen, modk[1])) + mm(chosen, modk[0])).astype(HALF)
        return carry

    lax.fori_loop(0, tokens // share, hidden_block, 0)
    gather.tick_until(list_q[-1])
    for piece in list_q:
        gather.arrive(piece)

    qkv_bias = jnp.concatenate([head_bias[i:i + 1, :] for i in range(3)], axis=1)

    def qkv_block(index, carry):
        rows = rows_at(index * share, share)
        values = mm(hid_a[rows, :], wq_full[...]) + qkv_bias
        for head in range(3 * nheads):
            heads[head, rows, :] = values[:, head * HD:(head + 1) * HD].astype(HALF)
        return carry

    lax.fori_loop(0, tokens // share, qkv_block, 0)

    def attend(block):
        start = block * share
        rows = rows_at(start, share)
        first = pl.multiple_of(jnp.clip(start - SEG_MOST, 0, tokens - window), 128)
        keys = pl.ds(first, window)

        def one_head(head, carry):
            same = seg_col[rows, :] == seg_row[:, keys]
            scores = mm_nt(heads[head, rows, :], heads[nheads + head, keys, :]) * (1.0 / math.sqrt(HD))
            scores = jnp.where(same, scores, -1e30)
            top = jnp.max(scores, axis=-1, keepdims=True)
            expo = jnp.exp(scores - top)
            total = jnp.sum(expo, axis=-1, keepdims=True)
            probs = (expo * (1.0 / total)).astype(HALF)
            att_heads[head, :, :] = mm(probs, heads[2 * nheads + head, keys, :])
            lse_heads[head] = top + jnp.log(total)
            return carry

        lax.fori_loop(0, nheads, one_head, 0)
        joined = jnp.concatenate([att_heads[head] for head in range(nheads)], axis=1).astype(HALF)
        att[rows, :] = joined
        lse[rows, :] = jnp.concatenate([lse_heads[head] for head in range(nheads)], axis=1)
        return joined

    def core_copy(slot, src):
        return remote(src, core_in.at[slot], sum_send.at[slot], sum_recv.at[slot], at.core_peer())

    y_copy = remote(y_out, y_in, sum_send.at[2], sum_recv.at[2], at.y_peer())

    gather.tick_until(list_p[0])
    joined = attend(at.share_of(True, True))
    gather.arrive(list_p[0])
    wp_tight[...] = mm(proj_place[...], wp_full[...]).astype(HALF)
    part[0] = mm(joined, wp_tight[...]).astype(HALF)
    core_copy(0, part.at[0]).start()
    gather.tick_until(list_i[0])
    joined = attend(at.share_of(False, True))
    part[1] = mm(joined, wp_tight[...]).astype(HALF)
    core_copy(1, part.at[1]).start()
    joined = attend(at.share_of(True, False))
    summed = mm(joined, wp_tight[...])
    core_copy(0, part.at[0]).wait_recv()
    y_out[...] = (summed + core_in[0].astype(FLOAT)).astype(HALF)
    y_copy.start()
    joined = attend(at.share_of(False, False))
    summed = mm(joined, wp_tight[...])
    core_copy(1, part.at[1]).wait_recv()
    summed = summed + core_in[1].astype(FLOAT)
    gather.tick_until(list_i[0] + 1)
    y_copy.wait_recv()
    branch[...] = summed + y_in[...].astype(FLOAT) + shared_bias[0:1, :]

    own_rows = rows_at(at.tensor * share, share)
    chosen = pick(own_rows)
    middle[...] = x_ref[own_rows, :].astype(FLOAT) + mm(chosen, modk[2]) * branch[...]
    normed, _ = layer_norm(middle[...])
    hid_b[own_rows, :] = (normed * (1.0 + mm(chosen, modk[4])) + mm(chosen, modk[3])).astype(HALF)

    def hid_rows(other_y, other_core):
        return hid_b.at[rows_at(at.share_of(other_y, other_core) * share, share)]

    own_hid = hid_rows(False, False)
    to_core = remote(own_hid, own_hid, gat_send.at[0], gat_recv.at[0], at.core_peer())
    to_y = remote(own_hid, own_hid, gat_send.at[1], gat_recv.at[1], at.y_peer())
    to_y.start()
    to_core.start()
    across = hid_rows(True, False)
    onward = remote(across, across, gat_send.at[2], gat_recv.at[2], at.core_peer())
    gather.tick_until(list_i[-1])
    remote(across, across, gat_send.at[1], gat_recv.at[1], at.y_peer()).wait_recv()
    onward.start()
    for piece in list_i:
        gather.arrive(piece)
    beside = hid_rows(False, True)
    remote(beside, beside, gat_send.at[0], gat_recv.at[0], at.core_peer()).wait_recv()
    far = hid_rows(True, True)
    remote(far, far, gat_send.at[2], gat_recv.at[2], at.core_peer()).wait_recv()
    gather.tick_until(list_o[0])

    def inner_block(index, carry):
        rows = rows_at(index * share, share)
        pre = mm(hid_b[rows, :], wi_full[...]) + inner_bias[...].reshape(1, -1)
        factor = math.sqrt(2.0 / math.pi)
        squared = pre * pre
        bend = jnp.tanh(factor * (pre + 0.044715 * squared * pre))
        act[rows, :] = (0.5 * pre * (1.0 + bend)).astype(HALF)
        slope[rows, :] = (
            0.5 * (1.0 + bend)
            + 0.5 * pre * (1.0 - bend * bend) * (factor * (1.0 + (3 * 0.044715) * squared))
        ).astype(HALF)
        return carry

    lax.fori_loop(0, tokens // share // 2, inner_block, 0)
    gather.tick_until(list_o[0] + 1)
    lax.fori_loop(tokens // share // 2, tokens // share, inner_block, 0)

    saves = []

    def save(src, dst):
        copy = pltpu.make_async_copy(src, dst, save_sem.at[len(saves)])
        copy.start()
        saves.append(copy)

    for src, dst in (
        (wq_full, wq_out), (wp_tight, wp_out), (wi_full, wi_out), (hid_a, hid_a_out), (heads, heads_out),
        (lse, lse_out), (att, att_out), (hid_b, hid_b_out), (act, act_out), (slope, slope_out),
        (branch, branch_out), (middle, middle_out), (modk, modk_out),
    ):
        save(src, dst)
    gather.tick_until(list_o[-1])
    for piece in list_o:
        gather.arrive(piece)
    save(wo_full, wo_out)

    def outer_block(other_y, other_core):
        rows = rows_at(at.share_of(other_y, other_core) * share, share)
        return mm(act[rows, :], wo_full[...])

    def ff_copy(slot):
        return remote(ff_part.at[slot], ff_in.at[slot], ff_send.at[slot], ff_recv.at[slot], at.core_peer())

    ff_part[0] = outer_block(True, True).astype(HALF)
    ff_copy(0).start()
    ff_part[1] = outer_block(False, True).astype(HALF)
    ff_copy(1).start()
    summed = outer_block(True, False)
    ff_copy(0).wait_recv()
    ff_far[...] = (summed + ff_in[0].astype(FLOAT)).astype(HALF)
    save(ff_far, far_out)
    summed = outer_block(False, False)
    ff_copy(1).wait_recv()
    ff_own[...] = summed + ff_in[1].astype(FLOAT)
    save(ff_own, own_out)
    ff_copy(0).wait_send()
    ff_copy(1).wait_send()

    for step in range(1, at.tensor_count):
        mod_copy(step).wait_send()
    core_copy(0, part.at[0]).wait_send()
    core_copy(1, part.at[1]).wait_send()
    y_copy.wait_send()
    to_core.wait_send()
    to_y.wait_send()
    onward.wait_send()
    for piece in range(last):
        gather.finish(piece)
    for copy in saves:
        copy.wait()


def any_spec():
    return pl.BlockSpec(memory_space=pl.ANY)


def vmem_spec():
    return pl.BlockSpec(memory_space=pltpu.VMEM)


def sizes_of(block_input, conditions, segment_ids, segment_cond, qkv_weight, inner_weight):
    dp_count, tensor_count = lax.axis_size(DP), lax.axis_size(TP)
    tokens, width = block_input.shape
    return {
        DP: dp_count,
        TP: tensor_count,
        "tokens": tokens,
        "rows": segment_ids.shape[0],
        "width": width,
        "columns": qkv_weight.shape[2],
        "hidden": inner_weight.shape[1],
        "shard": qkv_weight.shape[0],
        "share": tokens // tensor_count,
        "segs": segment_cond.shape[1],
        "conds": conditions.shape[0],
    }


def kernels_fit(sizes):
    return (
        sizes[TP] == 2 * CORES
        and sizes["rows"] == 1
        and sizes["share"] % 128 == 0
        and sizes["width"] % 128 == 0
        and sizes["hidden"] % 128 == 0
        and sizes["shard"] % 16 == 0
        and sizes["columns"] % 32 == 0
        and sizes["conds"] % (8 * sizes[TP]) == 0
    )


def placing(columns, own_rows, pad_rows, dp_count):
    tight = np.arange(columns)
    place = (tight // own_rows * pad_rows + tight % own_rows)[:, None] == np.arange(dp_count * pad_rows)
    return place.astype(np.float32)


def run_forward(sizes, block_input, seg_col, segment_ids, segment_cond, conditions, ada_weight, head_biases,
                inner_bias, shared_biases, wq, wp, wi, wo):
    tokens, width, columns, share = (sizes[k] for k in ("tokens", "width", "columns", "share"))
    hidden, dp_count, tensor_count = sizes["hidden"], sizes[DP], sizes[TP]
    nheads, segs = columns // HD, sizes["segs"]
    own_rows = columns // dp_count
    pad_rows = own_rows + -own_rows % 16
    shards = (sizes["shard"], pad_rows, sizes["shard"], hidden // dp_count)
    xs = line_length(dp_count)
    zs = dp_count // xs
    units = sum(shard // unit_rows(shard) for shard in shards)
    place = jnp.asarray(placing(columns, own_rows, pad_rows, dp_count), HALF)
    shapes = [
        ((width, 3 * columns), HALF), ((columns, width), HALF), ((width, hidden), HALF),
        ((hidden, width), HALF), ((tokens, width), HALF), ((3 * nheads, tokens, HD), HALF),
        ((tokens, nheads), FLOAT), ((tokens, columns), HALF), ((tokens, width), HALF),
        ((tokens, hidden), HALF), ((tokens, hidden), HALF), ((share, width), HALF), ((share, width), FLOAT),
        ((share, width), FLOAT), ((share, width), FLOAT), ((6, 2 * segs, width), HALF),
    ]
    vmem = pltpu.VMEM
    dma = pltpu.SemaphoreType.DMA
    scratch = [
        vmem((width, 3 * columns), HALF), vmem((dp_count * pad_rows, width), HALF),
        vmem((columns, width), HALF), vmem((width, hidden), HALF), vmem((hidden, width), HALF),
        vmem((tokens, width), HALF), vmem((3 * nheads, tokens, HD), HALF),
        vmem((tokens, nheads), FLOAT), vmem((nheads, share, 1), FLOAT), vmem((nheads, share, HD), FLOAT),
        vmem((tokens, columns), HALF), vmem((2, share, width), HALF), vmem((2, share, width), HALF),
        vmem((share, width), HALF), vmem((share, width), HALF), vmem((tokens, width), HALF),
        vmem((tokens, hidden), HALF), vmem((tokens, hidden), HALF), vmem((2, share, width), HALF),
        vmem((2, share, width), HALF), vmem((share, width), HALF), vmem((share, width), FLOAT),
        vmem((share, width), FLOAT), vmem((share, width), FLOAT), vmem((6, 2 * segs, width), HALF),
        vmem((tensor_count, 6, segs, columns), FLOAT), vmem((2, columns, width), FLOAT),
        vmem((pad_rows, width), FLOAT),
        dma((units, 2 * (zs - 1))), dma((units, 2 * (zs - 1))), dma((units, zs, xs - 1)),
        dma((units, zs, xs - 1)),
        dma((tensor_count - 1,)), dma((tensor_count - 1,)), dma((3,)), dma((3,)), dma((3,)), dma((3,)), dma((2,)), dma((2,)),
        dma((2,)), dma((16,)),
    ]
    return pl.pallas_call(
        functools.partial(forward_kernel, sizes),
        out_shape=[jax.ShapeDtypeStruct(s, t) for s, t in shapes],
        in_specs=[vmem_spec()] * 5 + [any_spec()] + [vmem_spec()] * 8,
        out_specs=[any_spec()] * len(shapes),
        scratch_shapes=scratch,
        name="forward",
        compiler_params=pltpu.CompilerParams(
            collective_id=1, has_side_effects=True, vmem_limit_bytes=VMEM_BYTES
        ),
    )(
        block_input, seg_col, segment_ids, segment_cond, conditions, ada_weight, head_biases, inner_bias,
        shared_biases, place, wq, wp, wi, wo,
    )


class Scatter:
    def __init__(self, place, pieces, x_sems, z_sems):
        self.place, self.pieces = place, pieces
        self.x_send, self.x_recv = x_sems
        self.z_send, self.z_recv = z_sems

    def slot(self, piece, z, x):
        whole, x_in, z_in, shard, first, count = self.pieces[piece]
        return whole.at[rows_at((z * self.place.xs + x) * shard + first, count)]

    def x_copy(self, piece, step, z):
        at = self.place
        whole, x_in, z_in, shard, first, count = self.pieces[piece]
        return remote(
            self.slot(piece, z, at.x_of(step)), x_in.at[step - 1, z, pl.ds(first, count)],
            self.x_send.at[piece, step - 1, z], self.x_recv.at[piece, step - 1, z], at.x_peer(step),
        )

    def z_copy(self, piece, step):
        at = self.place
        whole, x_in, z_in, shard, first, count = self.pieces[piece]
        return remote(
            self.slot(piece, at.z_of(step), at.x), z_in.at[step - 1, pl.ds(first, count)],
            self.z_send.at[piece, step - 1], self.z_recv.at[piece, step - 1], at.z_peer(step),
        )

    def start(self, piece):
        at = self.place
        for step in range(1, at.xs):
            for z in range(at.zs):
                self.x_copy(piece, step, z).start()

    def pass_on(self, piece):
        at = self.place
        whole, x_in, z_in, shard, first, count = self.pieces[piece]
        for z in range(at.zs):
            rows = rows_at((z * at.xs + at.x) * shard + first, count)
            total = whole[rows, :].astype(FLOAT)
            for step in range(1, at.xs):
                self.x_copy(piece, step, z).wait_recv()
                total = total + x_in[step - 1, z, first:first + count, :].astype(FLOAT)
            whole[rows, :] = total.astype(HALF)
        for step in sorted(range(1, at.zs), key=lambda s: -min(s, at.zs - s)):
            self.z_copy(piece, step).start()

    def arrive(self, piece):
        for step in range(1, self.place.zs):
            self.z_copy(piece, step).wait_recv()

    def finish(self, piece):
        at = self.place
        for step in range(1, at.xs):
            for z in range(at.zs):
                self.x_copy(piece, step, z).wait_send()
        for step in range(1, at.zs):
            self.z_copy(piece, step).wait_send()


class Spread:
    def __init__(self, place, chunks, z_sems, x_sems):
        self.place, self.chunks = place, chunks
        self.z_send, self.z_recv = z_sems
        self.x_send, self.x_recv = x_sems

    def z_copy(self, part, step, source):
        at = self.place
        chunk = self.chunks[part](self.place.z_of(source) * at.xs + at.x)
        return remote(chunk, chunk, self.z_send.at[part, step - 1], self.z_recv.at[part, step - 1], at.z_peer(step))

    def x_copy(self, part, back, step, source):
        at = self.place
        chunk = self.chunks[part](at.z_of(-back) * at.xs + at.x_of(source))
        sems = self.x_send.at[part, back, step - 1], self.x_recv.at[part, back, step - 1]
        return remote(chunk, chunk, *sems, at.x_peer(step))

    def start(self, part):
        for step in range(1, self.place.zs):
            self.z_copy(part, step, 0).start()

    def pass_on(self, part):
        for back in range(self.place.zs):
            if back > 0:
                self.z_copy(part, back, -back).wait_recv()
            for step in range(1, self.place.xs):
                self.x_copy(part, back, step, 0).start()

    def finish(self, part):
        at = self.place
        for step in range(1, at.zs):
            self.z_copy(part, step, 0).wait_send()
        for back in range(at.zs):
            for step in range(1, at.xs):
                self.x_copy(part, back, step, -step).wait_recv()
                self.x_copy(part, back, step, 0).wait_send()


def image_sums(chosen, values):
    high, low = split_two(values)
    return mm_tn(chosen, high) + mm_tn(chosen, low)


def backward_kernel(
    sizes,
    seg_col, seg_row, seg_cond, shared_bias, place_back,
    x_in, cot_in, wq_in, wp_in, wi_in, wo_in, hid_a_in, heads_in, lse_in, att_in, hid_b_in, act_in, slope_in,
    far_in, own_in, branch_in, middle_in, modk_in,
    block_out, input_out, qkv_out, proj_out, inner_out, outer_out, mods_out, packs_out, picks_out,
    wq, wp, wi, wo, heads, lse, att, hid_b, act, slope, cot, modk, branch, middle, ff_own,
    cot_own, x_own, gatt, key_sum, value_sum, grad_a, part, core_in, y_out, y_in, ff_in, grad_mid,
    whole_o, whole_i, whole_p, whole_q, xin_o, xin_i, xin_p, xin_q, zin_o, zin_i, zin_p, zin_q,
    mod_send_buf, mod_in, mods, packs, picks,
    load_sem, save_sem, x_send, x_recv, z_send, z_recv, sum_send, sum_recv, gat_send, gat_recv,
    ff_send, ff_recv, mod_send, mod_recv, all_z_send, all_z_recv, all_x_send, all_x_recv,
):
    at = Place(sizes[DP], sizes[TP])
    tokens, width, columns, share = sizes["tokens"], sizes["width"], sizes["columns"], sizes["share"]
    hidden = sizes["hidden"]
    nheads, segs = columns // HD, sizes["segs"]
    blocks = tokens // share
    scale = 1.0 / math.sqrt(HD)

    own_rows = rows_at(at.tensor * share, share)
    loads = {}

    def load(name, src, dst):
        copy = pltpu.make_async_copy(src, dst, load_sem.at[len(loads)])
        copy.start()
        loads[name] = copy

    load("cot", cot_in, cot)
    load("modk", modk_in, modk)
    load("act", act_in, act)
    load("wo", wo_in, wo)
    load("slope", slope_in, slope)
    load("wi", wi_in, wi)
    load("hid_b", hid_b_in, hid_b)
    load("middle", middle_in, middle)
    load("branch", branch_in, branch)
    load("ff_own", own_in, ff_own)
    load("att", att_in, att)
    load("wp", wp_in, wp)
    load("heads", heads_in, heads)
    load("lse", lse_in, lse)
    load("wq", wq_in, wq)
    load("x", x_in.at[own_rows], x_own)
    greet(
        [at.z_peer(s) for s in range(1, at.zs)]
        + [at.x_peer(s) for s in range(1, at.xs)]
        + [at.tensor_peer(s) for s in range(1, at.tensor_count)]
    )
    ff_copy = remote(far_in, ff_in, ff_send, ff_recv, at.y_peer())
    ff_copy.start()

    pieces = []
    for whole, x_in, z_in in (
        (whole_o, xin_o, zin_o), (whole_i, xin_i, zin_i), (whole_p, xin_p, zin_p), (whole_q, xin_q, zin_q)
    ):
        shard = x_in.shape[2]
        unit = unit_rows(shard)
        pieces.append([(whole, x_in, z_in, shard, first, unit) for first in range(0, shard, unit)])
    flat = [piece for group in pieces for piece in group]
    scatter = Scatter(at, flat, (x_send, x_recv), (z_send, z_recv))
    bounds = [sum(len(g) for g in pieces[:i]) for i in range(len(pieces) + 1)]
    list_o, list_i, list_p, list_q = (list(range(bounds[i], bounds[i + 1])) for i in range(4))

    def one_hot(rows, count):
        lanes = lax.broadcasted_iota(jnp.int32, (1, count), 1)
        return (seg_col[rows, :] == lax.rem(lanes, segs)).astype(FLOAT).astype(HALF)

    loads["cot"].wait()
    loads["modk"].wait()
    cot_own[...] = cot[own_rows, :]
    packs[at.dp] = jnp.zeros_like(packs[at.dp])
    picks[at.dp] = jnp.zeros_like(picks[at.dp])

    def grad_b_block(index, total):
        rows = rows_at(index * share, share)
        gate = mm(one_hot(rows, 2 * segs), modk[5])
        value = (cot[rows, :].astype(FLOAT) * gate).astype(HALF)
        cot[rows, :] = value
        return total + jnp.sum(value.astype(FLOAT), axis=0, keepdims=True)

    packs[at.dp, 3:4, 0:width] = lax.fori_loop(0, blocks, grad_b_block, jnp.zeros((1, width), FLOAT))
    loads["act"].wait()

    def lanes_at(index):
        return pl.ds(pl.multiple_of(index * 128, 128), 128)

    def outer_grad_block(index, carry):
        whole_o[rows_at(index * 128, 128), :] = mm_tn(act[:, lanes_at(index)], cot[...]).astype(HALF)
        return carry

    lax.fori_loop(0, hidden // 128, outer_grad_block, 0)
    for piece in list_o:
        scatter.start(piece)
    load("hid_a", hid_a_in, act)
    loads["wo"].wait()
    loads["slope"].wait()
    loads["wi"].wait()

    def back_two(block):
        rows = rows_at(block * share, share)
        grad_act = mm_nt(cot[rows, :], wo[...])
        grad_pre = (grad_act * slope[rows, :].astype(FLOAT)).astype(HALF)
        slope[rows, :] = grad_pre
        return mm_nt(grad_pre, wi[...]), jnp.sum(grad_pre.astype(FLOAT), axis=0, keepdims=True)

    def core_copy(slot):
        return remote(part.at[slot], core_in.at[slot], sum_send.at[slot], sum_recv.at[slot], at.core_peer())

    y_copy = remote(y_out, y_in, sum_send.at[2], sum_recv.at[2], at.y_peer())

    def sum_shares(make, between, held):
        part[0] = make(at.share_of(True, True)).astype(HALF)
        core_copy(0).start()
        part[1] = make(at.share_of(False, True)).astype(HALF)
        core_copy(1).start()
        summed = make(at.share_of(True, False))
        core_copy(0).wait_recv()
        y_out[...] = (summed + core_in[0].astype(FLOAT)).astype(HALF)
        y_copy.start()
        summed = make(at.share_of(False, False))
        core_copy(1).wait_recv()
        held[...] = summed + core_in[1].astype(FLOAT)
        between()
        y_copy.wait_recv()
        core_copy(0).wait_send()
        core_copy(1).wait_send()
        y_copy.wait_send()
        return held[...] + y_in[...].astype(FLOAT)

    bias_total = [jnp.zeros((1, hidden), FLOAT)]

    def make_two(block):
        value, bias = back_two(block)
        bias_total[0] = bias_total[0] + bias
        return value

    def inner_grads():
        packs[at.dp, 1:2, 0:hidden] = bias_total[0]
        loads["hid_b"].wait()

        def inner_grad_block(index, carry):
            whole_i[rows_at(index * 128, 128), :] = mm_tn(hid_b[:, lanes_at(index)], slope[...]).astype(HALF)
            return carry

        lax.fori_loop(0, width // 128, inner_grad_block, 0)
        for piece in list_i:
            scatter.start(piece)
        for piece in list_o[:2]:
            scatter.pass_on(piece)

    grad_hid_b = sum_shares(make_two, inner_grads, grad_mid)

    loads["middle"].wait()
    loads["branch"].wait()
    loads["ff_own"].wait()
    chosen = one_hot(own_rows, 2 * segs)
    normed, inv_std = layer_norm(middle[...])
    grad_normed = grad_hid_b * (1.0 + mm(chosen, modk[4]))
    first_mean = jnp.mean(grad_normed, axis=-1, keepdims=True)
    second_mean = jnp.mean(grad_normed * normed, axis=-1, keepdims=True)
    grad_mid[...] = cot_own[...].astype(FLOAT) + inv_std * (grad_normed - first_mean - normed * second_mean)
    grad_a[own_rows, :] = (grad_mid[...] * mm(chosen, modk[2])).astype(HALF)

    def hid_rows(other_y, other_core):
        return grad_a.at[rows_at(at.share_of(other_y, other_core) * share, share)]

    own_hid = hid_rows(False, False)
    to_core = remote(own_hid, own_hid, gat_send.at[0], gat_recv.at[0], at.core_peer())
    to_y = remote(own_hid, own_hid, gat_send.at[1], gat_recv.at[1], at.y_peer())
    to_y.start()
    to_core.start()
    across, beside, far = hid_rows(True, False), hid_rows(False, True), hid_rows(True, True)
    onward = remote(across, across, gat_send.at[2], gat_recv.at[2], at.core_peer())

    images = one_hot(own_rows, segs)

    def keep_mod(group, values):
        sums = image_sums(images, values)
        for t in range(at.tensor_count):
            mod_send_buf[t, group] = sums[:, t * columns:(t + 1) * columns]

    keep_mod(2, grad_mid[...] * branch[...])
    keep_mod(3, grad_hid_b)
    keep_mod(4, grad_hid_b * normed)
    mod_parts = ((2, 4), (0, 2))
    spread = Spread(
        at,
        [
            lambda source: mods.at[source, pl.ds(2, 4)],
            lambda source: mods.at[source, pl.ds(0, 2)],
            lambda source: packs.at[source],
            lambda source: picks.at[source],
        ],
        (all_z_send, all_z_recv), (all_x_send, all_x_recv),
    )

    def mod_copy(part_index, step):
        first, count = mod_parts[part_index]
        to = lax.rem(at.tensor + step, at.tensor_count)
        return remote(
            mod_send_buf.at[to, pl.ds(first, count)], mod_in.at[step - 1, pl.ds(first, count)],
            mod_send.at[part_index, step - 1], mod_recv.at[part_index, step - 1], at.tensor_peer(step),
        )

    def mod_start(part_index):
        for step in range(1, at.tensor_count):
            mod_copy(part_index, step).start()

    def mod_spread(part_index):
        first, count = mod_parts[part_index]
        total = mod_send_buf[at.tensor, first:first + count]
        for step in range(1, at.tensor_count):
            mod_copy(part_index, step).wait_recv()
            total = total + mod_in[step - 1, first:first + count]
        mods[at.dp, first:first + count] = total
        spread.start(part_index)

    window = min(tokens, share + 2 * SEG_MOST)
    key_sum[...] = jnp.zeros_like(key_sum)
    value_sum[...] = jnp.zeros_like(value_sum)

    def grad_att(block):
        rows = rows_at(block * share, share)
        values = mm_nt(grad_a[rows, :], wp[...])
        for head in range(nheads):
            gatt[head] = values[:, head * HD:(head + 1) * HD].astype(HALF)
        return jnp.sum(grad_a[rows, :].astype(FLOAT), axis=0, keepdims=True)

    def attend_back(block):
        start = block * share
        rows = rows_at(start, share)
        keys_at = pl.ds(pl.multiple_of(jnp.clip(start - SEG_MOST, 0, tokens - window), 128), window)

        def one_head(head, carry):
            query = heads[head, rows, :]
            keys = heads[nheads + head, keys_at, :]
            values = heads[2 * nheads + head, keys_at, :]
            grad = gatt[head]
            same = seg_col[rows, :] == seg_row[:, keys_at]
            scores = jnp.where(same, mm_nt(query, keys) * scale, -1e30)
            lanes = lax.broadcasted_iota(jnp.int32, (1, nheads), 1)
            peak = jnp.sum(jnp.where(lanes == head, lse[rows, :], 0.0), axis=-1, keepdims=True)
            probs = jnp.exp(scores - peak)
            grad_probs = mm_nt(grad, values)
            center = jnp.sum(probs * grad_probs, axis=-1, keepdims=True)
            grad_scores = (probs * (grad_probs - center)).astype(HALF)
            heads[head, rows, :] = (mm(grad_scores, keys) * scale).astype(HALF)
            key_sum[head, keys_at, :] += mm_tn(grad_scores, query)
            value_sum[head, keys_at, :] += mm_tn(probs.astype(HALF), grad)
            return carry

        lax.fori_loop(0, nheads, one_head, 0)

    loads["wp"].wait()
    loads["heads"].wait()
    loads["lse"].wait()
    grad_a_sum = grad_att(at.share_of(False, False))
    attend_back(at.share_of(False, False))
    for piece in list_o[2:]:
        scatter.pass_on(piece)
    remote(beside, beside, gat_send.at[0], gat_recv.at[0], at.core_peer()).wait_recv()
    grad_a_sum = grad_a_sum + grad_att(at.share_of(False, True))
    remote(across, across, gat_send.at[1], gat_recv.at[1], at.y_peer()).wait_recv()
    onward.start()
    attend_back(at.share_of(False, True))
    grad_a_sum = grad_a_sum + grad_att(at.share_of(True, False))
    attend_back(at.share_of(True, False))
    scatter.pass_on(list_i[0])
    remote(far, far, gat_send.at[2], gat_recv.at[2], at.core_peer()).wait_recv()
    grad_a_sum = grad_a_sum + grad_att(at.share_of(True, True))
    attend_back(at.share_of(True, True))
    packs[at.dp, 2:3, 0:width] = grad_a_sum
    loads["att"].wait()
    proj_grad = mm_tn(att[...], grad_a[...]).astype(HALF)
    whole_p[...] = mm(place_back[...], proj_grad).astype(HALF)
    for piece in list_p:
        scatter.start(piece)
    to_core.wait_send()
    to_y.wait_send()
    onward.wait_send()

    def join_block(index, total):
        rows = rows_at(index * share, share)
        parts = [heads[head, rows, :].astype(FLOAT) for head in range(nheads)]
        parts += [(key_sum[head, rows, :] * scale).astype(HALF).astype(FLOAT) for head in range(nheads)]
        parts += [value_sum[head, rows, :].astype(HALF).astype(FLOAT) for head in range(nheads)]
        values = jnp.concatenate(parts, axis=1)
        grad_a[rows, 0:3 * columns] = values.astype(HALF)
        return total + jnp.sum(values, axis=0, keepdims=True)

    packs[at.dp, 0:1, 0:3 * columns] = lax.fori_loop(0, blocks, join_block, jnp.zeros((1, 3 * columns), FLOAT))
    for piece in list_i[1:2]:
        scatter.pass_on(piece)
    loads["hid_a"].wait()

    def qkv_grad_block(index, carry):
        whole_q[rows_at(index * 128, 128), :] = mm_tn(act[:, lanes_at(index)], grad_a[:, 0:3 * columns]).astype(HALF)
        return carry

    lax.fori_loop(0, width // 128, qkv_grad_block, 0)
    for piece in list_q:
        scatter.start(piece)
    loads["wq"].wait()

    saves = []

    def save(src, dst):
        copy = pltpu.make_async_copy(src, dst, save_sem.at[len(saves)])
        copy.start()
        saves.append(copy)

    def mod_sums():
        for piece in list_i[2:] + list_p:
            scatter.pass_on(piece)
        ff_copy.wait_recv()
        branch_b = ff_own[...] + ff_in[...].astype(FLOAT) + shared_bias[1:2, :]
        keep_mod(5, cot_own[...].astype(FLOAT) * branch_b)
        ff_in[...] = (middle[...] + mm(chosen, modk[5]) * branch_b).astype(HALF)
        save(ff_in, block_out)
        mod_start(0)
        for part_index in (2, 3):
            spread.start(part_index)
        for piece in list_q[:1]:
            scatter.pass_on(piece)

    unit = lax.broadcasted_iota(jnp.int32, (segs, 1), 0) == lax.broadcasted_iota(jnp.int32, (1, segs), 1)
    conds = sizes["conds"]
    picks[at.dp, 0:segs, 0:conds] = mm_nt(unit.astype(FLOAT).astype(HALF), cond_picks(seg_cond, conds))
    grad_hid_a = sum_shares(
        lambda block: mm_nt(grad_a[rows_at(block * share, share), 0:3 * columns], wq[...]), mod_sums, branch
    )
    loads["x"].wait()
    normed, inv_std = layer_norm(x_own[...].astype(FLOAT))
    grad_normed = grad_hid_a * (1.0 + mm(chosen, modk[1]))
    first_mean = jnp.mean(grad_normed, axis=-1, keepdims=True)
    second_mean = jnp.mean(grad_normed * normed, axis=-1, keepdims=True)
    grad_mid[...] = grad_mid[...] + inv_std * (grad_normed - first_mean - normed * second_mean)
    save(grad_mid, input_out)
    mod_spread(0)
    keep_mod(0, grad_hid_a)
    keep_mod(1, grad_hid_a * normed)
    mod_start(1)
    for piece in list_q[1:]:
        scatter.pass_on(piece)
    for part_index in (2, 3, 0):
        spread.pass_on(part_index)
    mod_spread(1)
    spread.pass_on(1)
    outs = ((list_o, outer_out), (list_i, inner_out), (list_p, proj_out), (list_q, qkv_out))
    for pieces_of, out in outs:
        whole, x_in, z_in, shard = flat[pieces_of[0]][:4]
        for piece in pieces_of:
            scatter.arrive(piece)
        save(whole.at[rows_at((at.z * at.xs + at.x) * shard, shard)], out.at[0])
        for step in range(1, at.zs):
            save(z_in.at[step - 1], out.at[step])
    for part_index in range(4):
        spread.finish(part_index)
    save(mods, mods_out)
    save(packs, packs_out)
    save(picks, picks_out)
    ff_copy.wait_send()
    for piece in range(len(flat)):
        scatter.finish(piece)
    for part_index in range(2):
        for step in range(1, at.tensor_count):
            mod_copy(part_index, step).wait_send()
    for copy in saves:
        copy.wait()


def run_backward(sizes, block_input, seg_col, segment_ids, segment_cond, shared_biases, cotangent, kept):
    (wq, wp, wi, wo, hid_a, heads, lse, att, hid_b, act, slope, far, own, branch, middle, modk) = kept
    tokens, width, columns, share = (sizes[k] for k in ("tokens", "width", "columns", "share"))
    hidden, dp_count, tensor_count, segs = sizes["hidden"], sizes[DP], sizes[TP], sizes["segs"]
    nheads = columns // HD
    own_rows = columns // dp_count
    pad_rows = own_rows + -own_rows % 16
    xs = line_length(dp_count)
    zs = dp_count // xs
    shards = (hidden // dp_count, width // dp_count, pad_rows, width // dp_count)
    wholes = ((hidden, width), (width, hidden), (dp_count * pad_rows, width), (width, 3 * columns))
    units = sum(shard // unit_rows(shard) for shard in shards)
    place = jnp.asarray(placing(columns, own_rows, pad_rows, dp_count).T, HALF)
    pack_width = max(width, hidden, 3 * columns)
    shapes = [((share, width), HALF), ((share, width), FLOAT)]
    shapes += [((zs, shards[i], wholes[i][1]), HALF) for i in (3, 2, 1, 0)]
    shapes += [((dp_count, 6, segs, columns), FLOAT), ((dp_count, 4, pack_width), FLOAT)]
    shapes += [((dp_count, 8, 128), FLOAT)]
    vmem, dma = pltpu.VMEM, pltpu.SemaphoreType.DMA
    scratch = [
        vmem((width, 3 * columns), HALF), vmem((columns, width), HALF), vmem((width, hidden), HALF),
        vmem((hidden, width), HALF), vmem((3 * nheads, tokens, HD), HALF), vmem((tokens, nheads), FLOAT),
        vmem((tokens, columns), HALF), vmem((tokens, width), HALF), vmem((tokens, hidden), HALF),
        vmem((tokens, hidden), HALF), vmem((tokens, width), HALF), vmem((6, 2 * segs, width), HALF),
        vmem((share, width), FLOAT), vmem((share, width), FLOAT), vmem((share, width), FLOAT),
        vmem((share, width), HALF), vmem((share, width), HALF), vmem((nheads, share, HD), HALF),
        vmem((nheads, tokens, HD), FLOAT), vmem((nheads, tokens, HD), FLOAT), vmem((tokens, width), HALF),
        vmem((2, share, width), HALF), vmem((2, share, width), HALF), vmem((share, width), HALF),
        vmem((share, width), HALF), vmem((share, width), HALF), vmem((share, width), FLOAT),
    ]
    scratch += [vmem(shape, HALF) for shape in wholes]
    scratch += [vmem((xs - 1, zs, shards[i], wholes[i][1]), HALF) for i in range(4)]
    scratch += [vmem((zs - 1, shards[i], wholes[i][1]), HALF) for i in range(4)]
    scratch += [
        vmem((tensor_count, 6, segs, columns), FLOAT), vmem((tensor_count - 1, 6, segs, columns), FLOAT),
        vmem((dp_count, 6, segs, columns), FLOAT), vmem((dp_count, 4, pack_width), FLOAT),
        vmem((dp_count, 8, 128), FLOAT),
        dma((17,)), dma((5 + 4 * zs,)), dma((units, xs - 1, zs)), dma((units, xs - 1, zs)),
        dma((units, zs - 1)), dma((units, zs - 1)), dma((3,)), dma((3,)), dma((3,)), dma((3,)),
        dma(()), dma(()), dma((2, tensor_count - 1)), dma((2, tensor_count - 1)),
        dma((4, zs - 1)), dma((4, zs - 1)), dma((4, zs, xs - 1)), dma((4, zs, xs - 1)),
    ]
    return pl.pallas_call(
        functools.partial(backward_kernel, sizes),
        out_shape=[jax.ShapeDtypeStruct(s, t) for s, t in shapes],
        in_specs=[vmem_spec()] * 5 + [any_spec()] * 18,
        out_specs=[any_spec()] * len(shapes),
        scratch_shapes=scratch,
        name="backward",
        compiler_params=pltpu.CompilerParams(
            collective_id=2, has_side_effects=True, vmem_limit_bytes=VMEM_BYTES
        ),
    )(
        seg_col, segment_ids, segment_cond, shared_biases, place, block_input, cotangent, wq, wp, wi, wo, hid_a, heads, lse, att, hid_b, act, slope, far, own,
        branch, middle, modk,
    )


def on_device_general(
    block_input,
    conditions,
    segment_ids,
    segment_cond,
    cotangent,
    qkv_weight,
    proj_weight,
    inner_weight,
    outer_weight,
    ada_weight,
    head_biases,
    inner_bias,
    shared_biases,
    qkv_first,
    proj_first,
    inner_first,
    outer_first,
    ada_first,
    head_biases_first,
    inner_bias_first,
    shared_biases_first,
    qkv_second,
    proj_second,
    inner_second,
    outer_second,
    ada_second,
    head_biases_second,
    inner_bias_second,
    shared_biases_second,
):
    columns = qkv_weight.shape[2]
    heads_local = columns // HD
    rows_local = segment_ids.shape[0]
    row_length = segment_ids.shape[1]
    token_count = rows_local * row_length
    seg_count = segment_cond.shape[1]
    width = block_input.shape[1]
    share_count = token_count // lax.axis_size(TP)
    share_start = lax.axis_index(TP) * share_count

    def share(values):
        return lax.dynamic_slice_in_dim(values, share_start, share_count, 0)

    qkv_full, proj_full, inner_full, outer_full = (
        lax.all_gather(qkv_weight.astype(HALF), DP, axis=0, tiled=True),
        lax.all_gather(proj_weight.astype(HALF), DP, axis=0, tiled=True),
        lax.all_gather(inner_weight.astype(HALF), DP, axis=0, tiled=True),
        lax.all_gather(outer_weight.astype(HALF), DP, axis=0, tiled=True),
    )
    condition_select = (
        segment_cond[:, :, None] == jnp.arange(conditions.shape[0])[None, None, :]
    ).astype(FLOAT)
    condition_row_block = jnp.einsum(
        "btu,ua->bta", condition_select, conditions, precision=PRECISION_MAX
    )
    cond_act = silu(condition_row_block)
    local_mod = (
        jnp.einsum("rsd,kcd->rskc", cond_act, ada_weight, precision=PRECISION_MAX)
        + head_biases[3:][None, None]
    )
    full_mod = lax.all_gather(local_mod, TP, axis=3, tiled=True)
    seg_pick = (segment_ids[:, :, None] == jnp.arange(seg_count)[None, None, :]).astype(FLOAT)
    token_mod = jnp.einsum("rls,rskd->rlkd", seg_pick, full_mod, precision=PRECISION_MAX).reshape(
        token_count, 6, width
    )
    inputs = block_input.astype(FLOAT)
    normed_one, inv_one = normalize(inputs)
    hidden_one = (normed_one * (1.0 + token_mod[:, 1]) + token_mod[:, 0]).astype(HALF)
    qkv_values = (
        jnp.einsum("nd,dkc->nkc", hidden_one, qkv_full, preferred_element_type=FLOAT)
        + head_biases[:3][None]
    ).astype(HALF)
    row_qkv = qkv_values.reshape(rows_local, row_length, 3, heads_local, HD)
    row = 0
    attended_row, total_row = attend_forward(row_qkv[row], segment_ids[row])
    attended_rows = [attended_row]
    total_rows = [total_row]
    attended = jnp.stack(attended_rows).reshape(token_count, columns).astype(HALF)
    attn_partial = jnp.dot(attended, proj_full, preferred_element_type=FLOAT)
    share_mod = share(token_mod)
    branch_one = sum_to_shares(attn_partial) + shared_biases[0]
    middle = share(inputs) + share_mod[:, 2] * branch_one
    normed_two, inv_two = normalize(middle)
    hidden_two_share = (normed_two * (1.0 + share_mod[:, 4]) + share_mod[:, 3]).astype(HALF)
    hidden_two = lax.all_gather(hidden_two_share, TP, axis=0, tiled=True)
    pre_act = jnp.dot(hidden_two, inner_full, preferred_element_type=FLOAT) + inner_bias
    act_values, gelu_back = jax.vjp(gelu_tanh, pre_act)
    act_low = act_values.astype(HALF)
    ff_partial = jnp.dot(act_low, outer_full, preferred_element_type=FLOAT)
    branch_two = sum_to_shares(ff_partial) + shared_biases[1]
    output = middle + share_mod[:, 5] * branch_two
    grad_out = cotangent.astype(FLOAT)
    grad_two = (grad_out * token_mod[:, 5]).astype(HALF)
    outer_grad = jnp.einsum("nf,nd->fd", act_low, grad_two, preferred_element_type=FLOAT)
    grad_act = jnp.einsum("nd,fd->nf", grad_two, outer_full, preferred_element_type=FLOAT)
    grad_pre = gelu_back(grad_act)[0].astype(HALF)
    inner_grad = jnp.einsum("nd,nf->df", hidden_two, grad_pre, preferred_element_type=FLOAT)
    back_two_partial = jnp.einsum("nf,df->nd", grad_pre, inner_full, preferred_element_type=FLOAT)
    grad_hidden_two = sum_to_shares(back_two_partial)
    grad_out_share = share(grad_out)
    grad_middle = grad_out_share + norm_back(
        grad_hidden_two * (1.0 + share_mod[:, 4]), normed_two, inv_two
    )
    grad_one_share = (grad_middle * share_mod[:, 2]).astype(HALF)
    grad_one = lax.all_gather(grad_one_share, TP, axis=0, tiled=True)
    proj_grad = jnp.einsum("nc,nd->cd", attended, grad_one, preferred_element_type=FLOAT)
    grad_attended = jnp.einsum(
        "nd,cd->nc", grad_one, proj_full, preferred_element_type=FLOAT
    ).astype(HALF)
    grad_rows = grad_attended.reshape(rows_local, row_length, heads_local, HD)
    row = 0
    grad_qkv_rows = [
        attend_backward(row_qkv[row], segment_ids[row], grad_rows[row], total_rows[row])
    ]
    grad_qkv = jnp.stack(grad_qkv_rows).reshape(token_count, 3, columns).astype(HALF)
    qkv_grad = jnp.einsum("nd,nkc->dkc", hidden_one, grad_qkv, preferred_element_type=FLOAT)
    back_one_partial = jnp.einsum("nkc,dkc->nd", grad_qkv, qkv_full, preferred_element_type=FLOAT)
    grad_hidden_one = sum_to_shares(back_one_partial)
    normed_one_share, inv_one_share = share(normed_one), share(inv_one)
    input_out = grad_middle + norm_back(
        grad_hidden_one * (1.0 + share_mod[:, 1]), normed_one_share, inv_one_share
    )
    block_out = output.astype(HALF)
    contributions = jnp.concatenate(
        [
            grad_hidden_one,
            grad_hidden_one * normed_one_share,
            grad_middle * branch_one,
            grad_hidden_two,
            grad_hidden_two * normed_two,
            grad_out_share * branch_two,
        ],
        axis=1,
    )
    pick_share = share(seg_pick.reshape(token_count, seg_count))
    cond_pick = jnp.dot(pick_share, condition_select[0], precision=PRECISION_MAX)
    cond_sums = jnp.einsum("lq,lc->qc", cond_pick, contributions, precision=PRECISION_MAX)
    cond_sums = cond_sums.reshape(-1, 6, lax.axis_size(TP), columns)
    cond_sums = lax.psum_scatter(cond_sums, TP, scatter_dimension=2, tiled=True)[:, :, 0]
    cond_total = lax.psum(cond_sums, DP)
    all_act, all_silu_back = jax.vjp(silu, conditions)
    grad_all_act = jnp.einsum("qkc,kcd->qd", cond_total, ada_weight, precision=PRECISION_MAX)
    cond_grad = all_silu_back(lax.psum(grad_all_act, TP))[0]
    head_bias_grad = jnp.sum(grad_qkv.astype(FLOAT), axis=0)
    inner_bias_grad = jnp.sum(grad_pre.astype(FLOAT), axis=0)
    shared_bias_grad = jnp.stack(
        [jnp.sum(grad_one.astype(FLOAT), axis=0), jnp.sum(grad_two.astype(FLOAT), axis=0)]
    )
    ada_total = jnp.einsum("qd,qkc->kcd", all_act, cond_total, precision=PRECISION_MAX)
    head_total, inner_bias_total, shared_total = lax.psum(
        (head_bias_grad, inner_bias_grad, shared_bias_grad), DP
    )
    head_total = jnp.concatenate([head_total, jnp.sum(cond_total, axis=0)], axis=0)
    qkv_shard, proj_shard, inner_shard, outer_shard = (
        sum_to_owners(qkv_grad),
        sum_to_owners(proj_grad),
        sum_to_owners(inner_grad),
        sum_to_owners(outer_grad),
    )
    qkv_new = adam_update(qkv_weight, qkv_shard, qkv_first, qkv_second, RATES[0])
    proj_new = adam_update(proj_weight, proj_shard, proj_first, proj_second, RATES[1])
    inner_new = adam_update(inner_weight, inner_shard, inner_first, inner_second, RATES[2])
    outer_new = adam_update(outer_weight, outer_shard, outer_first, outer_second, RATES[3])
    ada_new = adam_update(ada_weight, ada_total, ada_first, ada_second, RATES[4])
    head_new = adam_update(head_biases, head_total, head_biases_first, head_biases_second, RATES[5])
    inner_bias_new = adam_update(
        inner_bias, inner_bias_total, inner_bias_first, inner_bias_second, RATES[6]
    )
    shared_new = adam_update(
        shared_biases, shared_total, shared_biases_first, shared_biases_second, RATES[7]
    )
    return (
        block_out,
        input_out,
        cond_grad,
        qkv_new[0],
        proj_new[0],
        inner_new[0],
        outer_new[0],
        ada_new[0],
        head_new[0],
        inner_bias_new[0],
        shared_new[0],
        qkv_new[1],
        proj_new[1],
        inner_new[1],
        outer_new[1],
        ada_new[1],
        head_new[1],
        inner_bias_new[1],
        shared_new[1],
        qkv_new[2],
        proj_new[2],
        inner_new[2],
        outer_new[2],
        ada_new[2],
        head_new[2],
        inner_bias_new[2],
        shared_new[2],
        qkv_new[0].astype(HALF),
        proj_new[0].astype(HALF),
        inner_new[0].astype(HALF),
        outer_new[0].astype(HALF),
    )


def update_kernel(
    sizes,
    cond_ref, mods, packs, picks, head_w, head_m, head_v, hidden_w, hidden_m, hidden_v, shared_w, shared_m, shared_v,
    *refs,
):
    width, columns, segs, hidden = sizes["width"], sizes["columns"], sizes["segs"], sizes["hidden"]
    big_in = [refs[i * 4:i * 4 + 4] for i in range(4)]
    ada_in = refs[16:19]
    part, *small_out = refs[19:29]
    ada_out = refs[29:32]
    big_out = [refs[32 + i * 4:36 + i * 4] for i in range(4)]
    refs = refs[48:]
    ada = refs[:3]
    big = [refs[3 + i * 5:8 + i * 5] for i in range(4)]
    gt, act_rows, head_grad = refs[23:26]
    ada_load, ada_save, big_load, big_save = refs[26:]
    conds, dp_count = cond_ref.shape[0], sizes[DP]

    def ada_copy(kind, group):
        return pltpu.make_async_copy(ada_in[kind].at[group], ada[kind].at[group], ada_load.at[kind, group])

    for group in range(6):
        ada_copy(0, group).start()
    for group in range(6):
        ada_copy(1, group).start()
        ada_copy(2, group).start()
    big_loads = []
    for index in range(4):
        copies = [
            pltpu.make_async_copy(big_in[index][kind], big[index][kind], big_load.at[index, kind])
            for kind in range(4)
        ]
        for copy in copies:
            copy.start()
        big_loads.append(copies)

    act = silu(cond_ref[...])
    act_high, act_low = split_two(act)
    act_rows[...] = jnp.concatenate([act_high, act_high, act_low], axis=0)
    picked = jnp.concatenate(
        [picks[row, 0:segs, 0:conds] for row in range(dp_count)], axis=0
    ).astype(HALF)
    for group in range(6):
        images = jnp.concatenate([mods[row, group] for row in range(dp_count)], axis=0)
        head_grad[3 + group:4 + group, :] = jnp.sum(images, axis=0, keepdims=True)
        high, low = split_two(images)
        sums_high, sums_low = split_two(mm_tn(high, picked) + mm_tn(low, picked))
        gt[group] = jnp.concatenate([sums_high, sums_low, sums_high], axis=1)

    part[...] = jnp.zeros_like(part)
    for group in range(6):
        ada_copy(0, group).wait()
        weight_high, weight_low = split_two(ada[0][group])
        both = mm_tn(gt[group, :, 0:2 * conds], weight_high)
        part[...] += both[:conds] + both[conds:] + mm_tn(gt[group, :, 0:conds], weight_low)

    def update(values, rate, grad):
        weight, first, second = values
        return adam_update(weight, grad, first, second, rate)

    tile = 96 if columns % 96 == 0 else columns
    saves = []

    def ada_group(group):
        for kind in (1, 2):
            ada_copy(kind, group).wait()

        def ada_tile(index, carry):
            rows = pl.ds(pl.multiple_of(index * tile, 8), tile)
            grad = mm(gt[group, rows, :], act_rows[...])
            new = update([ref[group, rows, :] for ref in ada], RATES[4], grad)
            for ref, value in zip(ada, new, strict=True):
                ref[group, rows, :] = value
            return carry

        lax.fori_loop(0, columns // tile, ada_tile, 0)
        for kind in range(3):
            copy = pltpu.make_async_copy(ada[kind].at[group], ada_out[kind].at[group], ada_save.at[kind, group])
            copy.start()
            saves.append(copy)

    for group in range(6):
        ada_group(group)

    pack = packs[0]
    for row in range(1, dp_count):
        pack = pack + packs[row]
    for part_index in range(3):
        head_grad[part_index:part_index + 1, :] = pack[0:1, part_index * columns:(part_index + 1) * columns]
    smalls = (
        ((head_w, head_m, head_v), RATES[5], head_grad[...]),
        ((hidden_w, hidden_m, hidden_v), RATES[6], pack[1:2, 0:hidden].reshape(hidden_w.shape)),
        ((shared_w, shared_m, shared_v), RATES[7], pack[2:4, 0:width]),
    )
    for index, (kinds, rate, grad) in enumerate(smalls):
        for kind, value in enumerate(update([ref[...] for ref in kinds], rate, grad)):
            small_out[index * 3 + kind][...] = value

    for index in range(4):
        for copy in big_loads[index]:
            copy.wait()
        weight, first, second, grad, low = big[index]
        planes = weight.shape[0] if len(weight.shape) == 3 else 0
        for plane in range(max(planes, 1)):
            where = (plane,) if planes else (slice(0, weight.shape[0]),)
            lanes = weight.shape[-1]
            gradient = grad[0, :, plane * lanes:(plane + 1) * lanes].astype(FLOAT)
            for source in range(1, grad.shape[0]):
                gradient = gradient + grad[source, :, plane * lanes:(plane + 1) * lanes].astype(FLOAT)
            gradient = gradient[0:weight.shape[-2], :]
            new = update([ref[where] for ref in (weight, first, second)], RATES[index], gradient)
            for ref, value in zip((weight, first, second), new, strict=True):
                ref[where] = value
            low[where] = new[0].astype(HALF)
        for kind, ref in enumerate((weight, first, second, low)):
            copy = pltpu.make_async_copy(ref, big_out[index][kind], big_save.at[index, kind])
            copy.start()
            saves.append(copy)

    for copy in saves:
        copy.wait()


def run_update(sizes, conditions, mods, packs, picks, smalls, bigs, ada):
    width, columns, segs = sizes["width"], sizes["columns"], sizes["segs"]
    conds = conditions.shape[0]
    vmem, dma = pltpu.VMEM, pltpu.SemaphoreType.DMA
    flat_small = [array for kinds in smalls for array in kinds]
    flat_big = [array for kinds in bigs for array in kinds]

    def like(array, dtype=FLOAT):
        return jax.ShapeDtypeStruct(array.shape, dtype)

    outs = [like(conditions)] + [like(a) for a in flat_small] + [like(a) for a in ada]
    for weight, first, second, grad in bigs:
        outs += [like(weight), like(first), like(second), like(weight, HALF)]
    scratch = [vmem(array.shape, FLOAT) for array in ada]
    for kinds in bigs:
        scratch += [vmem(array.shape, array.dtype) for array in kinds] + [vmem(kinds[0].shape, HALF)]
    scratch += [
        vmem((6, columns, 3 * conds), HALF), vmem((3 * conds, width), HALF), vmem((9, columns), FLOAT),
        dma((3, 6)), dma((3, 6)), dma((4, 4)), dma((4, 4)),
    ]
    return pl.pallas_call(
        functools.partial(update_kernel, sizes),
        out_shape=outs,
        in_specs=[vmem_spec()] * 13 + [any_spec()] * 19,
        out_specs=[vmem_spec()] * 10 + [any_spec()] * 19,
        scratch_shapes=scratch,
        name="update",
        compiler_params=pltpu.CompilerParams(vmem_limit_bytes=VMEM_BYTES),
    )(conditions, mods, packs, picks, *flat_small, *flat_big, *ada)


def cond_kernel(sizes, cond_ref, part_in, cond_out, part, landing, result, out_send, out_recv, back_send, back_recv):
    at = Place(sizes[DP], sizes[TP])
    slice_rows = cond_ref.shape[0] // at.tensor_count
    part[...] = part_in[...]
    greet([at.tensor_peer(s) for s in range(1, at.tensor_count)])

    def slice_at(index):
        return pl.ds(pl.multiple_of(index * slice_rows, 8), slice_rows)

    def out_copy(step):
        to = lax.rem(at.tensor + step, at.tensor_count)
        return remote(
            part.at[slice_at(to)], landing.at[step - 1], out_send.at[step - 1], out_recv.at[step - 1],
            at.tensor_peer(step),
        )

    def back_copy(step, owner):
        rows = result.at[slice_at(owner)]
        return remote(rows, rows, back_send.at[step - 1], back_recv.at[step - 1], at.tensor_peer(step))

    for step in range(1, at.tensor_count):
        out_copy(step).start()

    total = part[slice_at(at.tensor), :]
    for step in range(1, at.tensor_count):
        out_copy(step).wait_recv()
        total = total + landing[step - 1]
    own = cond_ref[slice_at(at.tensor), :]
    gate = 1.0 / (1.0 + jnp.exp(-own))
    result[slice_at(at.tensor), :] = total * (gate * (1.0 + own * (1.0 - gate)))
    for step in range(1, at.tensor_count):
        back_copy(step, at.tensor).start()
    for step in range(1, at.tensor_count):
        back_copy(step, lax.rem(at.tensor + at.tensor_count - step, at.tensor_count)).wait_recv()
    cond_out[...] = result[...]
    for step in range(1, at.tensor_count):
        out_copy(step).wait_send()
        back_copy(step, at.tensor).wait_send()


def run_cond(sizes, conditions, part):
    tensor_count, vmem, dma = sizes[TP], pltpu.VMEM, pltpu.SemaphoreType.DMA
    shape = conditions.shape
    return pl.pallas_call(
        functools.partial(cond_kernel, sizes),
        out_shape=jax.ShapeDtypeStruct(shape, FLOAT),
        in_specs=[vmem_spec()] * 2,
        out_specs=vmem_spec(),
        scratch_shapes=[
            vmem(shape, FLOAT), vmem((tensor_count - 1, shape[0] // tensor_count, shape[1]), FLOAT),
            vmem(shape, FLOAT), *[dma((tensor_count - 1,))] * 4,
        ],
        name="cond",
        compiler_params=pltpu.CompilerParams(collective_id=3, has_side_effects=True),
    )(conditions, part)


def on_device_kernels(
    block_input, conditions, segment_ids, segment_cond, cotangent, qkv_weight, proj_weight, inner_weight,
    outer_weight, ada_weight, head_biases, inner_bias, shared_biases, *moments,
):
    firsts, seconds = moments[:8], moments[8:]
    sizes = sizes_of(block_input, conditions, segment_ids, segment_cond, qkv_weight, inner_weight)
    seg_col = segment_ids.reshape(-1, 1)

    def planes(array):
        return array.transpose(1, 0, 2)

    kept = run_forward(
        sizes, block_input, seg_col, segment_ids, segment_cond, conditions, ada_weight, head_biases, inner_bias,
        shared_biases, planes(qkv_weight), proj_weight, inner_weight, outer_weight,
    )
    block_out, input_out, *grads, mods, packs, picks = run_backward(
        sizes, block_input, seg_col, segment_ids, segment_cond, shared_biases, cotangent, kept
    )
    weights = (qkv_weight, proj_weight, inner_weight, outer_weight)
    bigs = [[w, m, v, g] for w, m, v, g in zip(weights, firsts[:4], seconds[:4], grads, strict=True)]
    bigs[0][:3] = [planes(array) for array in bigs[0][:3]]
    smalls = list(zip((head_biases, inner_bias, shared_biases), firsts[5:], seconds[5:], strict=True))
    cond_part, *news = run_update(
        sizes, conditions, mods, packs, picks, smalls, bigs, (ada_weight, firsts[4], seconds[4])
    )
    small_new, ada_new, big_new = news[:9], news[9:12], news[12:]
    big_new[:4] = [planes(array) for array in big_new[:4]]
    outs = [block_out, input_out, run_cond(sizes, conditions, cond_part)]
    for kind in range(3):
        outs += [big_new[4 * i + kind] for i in range(4)]
        outs += [ada_new[kind]] + [small_new[3 * i + kind] for i in range(3)]
    return (*outs, *big_new[3::4])


def on_device(*args):
    sizes = sizes_of(args[0], args[1], args[2], args[3], args[5], args[7])
    return (on_device_kernels if kernels_fit(sizes) else on_device_general)(*args)


def solution(mesh):
    in_specs = (
        P(DP, None),
        P(),
        P(DP, None),
        P(DP, None),
        P(DP, None),
        P(DP, None, TP),
        P((TP, DP), None),
        P(DP, TP),
        P((TP, DP), None),
        P(None, TP, None),
        P(None, TP),
        P(TP),
        P(),
        P(DP, None, TP),
        P((TP, DP), None),
        P(DP, TP),
        P((TP, DP), None),
        P(None, TP, None),
        P(None, TP),
        P(TP),
        P(),
        P(DP, None, TP),
        P((TP, DP), None),
        P(DP, TP),
        P((TP, DP), None),
        P(None, TP, None),
        P(None, TP),
        P(TP),
        P(),
    )
    out_specs = (
        P((DP, TP), None),
        P((DP, TP), None),
        P(),
        P(DP, None, TP),
        P((TP, DP), None),
        P(DP, TP),
        P((TP, DP), None),
        P(None, TP, None),
        P(None, TP),
        P(TP),
        P(),
        P(DP, None, TP),
        P((TP, DP), None),
        P(DP, TP),
        P((TP, DP), None),
        P(None, TP, None),
        P(None, TP),
        P(TP),
        P(),
        P(DP, None, TP),
        P((TP, DP), None),
        P(DP, TP),
        P((TP, DP), None),
        P(None, TP, None),
        P(None, TP),
        P(TP),
        P(),
        P(DP, None, TP),
        P((TP, DP), None),
        P(DP, TP),
        P((TP, DP), None),
    )
    return jax.shard_map(
        on_device, mesh=mesh, in_specs=in_specs, out_specs=out_specs, check_vma=False
    )
```

profile of v0, /device:TPU:0, one launch (start us, length us, event | category | flops | bytes accessed | tf_op | source)
XLA Modules:
  0.0 286.5 jit_solution(6095507244500240795)
XLA Ops:
  0.7 1.7 copy.63.seg_col
  2.4 118.7 %forward.1 = (bf16[1152,864]{1,0:T(8,128)(2,1)}, bf16[288,1152]{1,0:T(8,128)(2,1)}, bf16[1152,1152]{1,0:T(8,128)(2,1)}, bf16[1152,1152]{1,0:T(8,128)(2,1)}, bf16...) custom-call(bf16[1024,1152]{1,0:T(8,128)(2,1)} %x_in.1, ...), custom_call_target="tpu_custom_call" | custom-call | tf_op jit(solution)/shard_map/forward/pallas_call | solution.py:704
  121.1 129.1 %backward.1 = (bf16[256,1152]{1,0:T(8,128)(2,1)}, f32[256,1152]{1,0:T(8,128)}, bf16[4,144,864]{2,1,0:T(8,128)(2,1)}, bf16[4,48,1152]{2,1,0:T(8,128)(2,1)}, bf16[...) custom-call(s32[1024,1]{1,0:T(8,128)} %copy.63.seg_col, ...), custom_call_target="tpu_custom_call" | custom-call | tf_op jit(solution)/shard_map/backward/pallas_call | solution.py:1235
  250.2 0.0 copy-start.2
  250.2 24.7 %update.1 = (f32[32,1152]{1,0:T(8,128)}, f32[9,288]{1,0:T(8,128)}, f32[9,288]{1,0:T(8,128)}, f32[9,288]{1,0:T(8,128)}, f32[1152]{0:T(1024)}, /*index=5*/f32[1152...) custom-call(f32[32,1152]{1,0:T(8,128)} %cond_ref.5, ...), custom_call_target="tpu_custom_call" | custom-call | tf_op jit(solution)/shard_map/update/pallas_call | solution.py:1601
  274.9 0.0 copy-start
  274.9 8.7 %cond.1 = f32[32,1152]{1,0:T(8,128)} custom-call(f32[32,1152]{1,0:T(8,128)} %cond_ref.5, f32[32,1152]{1,0:T(8,128)} %get-tuple-element.110.part_in), custom_call_target="tpu_custom_call" | custom-call | tf_op jit(solution)/shard_map/cond/pallas_call | solution.py:1655
  283.7 0.0 copy-start.1
  283.7 0.0 copy-done.2
  283.7 0.8 copy.67
  284.5 0.0 copy-done
  284.5 1.0 copy.68
  285.5 0.0 copy-done.1
  285.6 0.7 copy.69
Async XLA Ops:
  250.2 33.5 %copy-start.2 = (bf16[256,1152]{1,0:T(8,128)(2,1)S(1)}, bf16[256,1152]{1,0:T(8,128)(2,1)}, u32[]{:S(2)}) copy-start(bf16[256,1152]{1,0:T(8,128)(2,1)} %get-tuple-element.170) | copy-start | bytes 1769476
  274.9 9.6 %copy-start = (f32[256,1152]{1,0:T(8,128)S(1)}, f32[256,1152]{1,0:T(8,128)}, u32[]{:S(2)}) copy-start(f32[256,1152]{1,0:T(8,128)} %get-tuple-element.171) | copy-start | bytes 3538948
  283.7 1.9 copy-start.1
where the time goes:
time: 289 us; the launch traced here: 286 us
  Pallas kernels  281 us (97%)
  local copies, waits for them, and re-layouts  4.21 us (1%)
    pallas_call x1, Pallas kernels, run_backward(): pl.pallas_call(functools.partial(backward_kernel, sizes), out_shape=[jax....  129 us
    pallas_call x1, Pallas kernels, run_forward(): pl.pallas_call(functools.partial(forward_kernel, sizes), out_shape=[jax.S...  119 us
    pallas_call x1, Pallas kernels, run_update(): pl.pallas_call(functools.partial(update_kernel, sizes), out_shape=outs, i...  24.7 us
    pallas_call x1, Pallas kernels, run_cond(): pl.pallas_call(functools.partial(cond_kernel, sizes), out_shape=jax.Shape...  8.74 us

commit v1 on v0

--- a/solution.py
+++ b/solution.py
@@ -242,8 +242,14 @@
     return pl.ds(pl.multiple_of(start, 16), count)
 
 
-def unit_rows(shard):
-    return 48 if shard % 48 == 0 else shard
+AHEAD = 3
+
+
+def unit_rows(shard, most=48):
+    return most if shard % most == 0 else shard
+
+
+FIRST_UNIT, LAST_UNIT = 48, 48
 
 
 class Gather:
@@ -318,8 +324,8 @@
         for away in range(1, self.hops + 1):
             if 0 <= now - away + 1 < len(self.pieces):
                 self.pass_on(now - away + 1, away)
-        if now + 3 < len(self.pieces):
-            self.start(now + 3)
+        if now + AHEAD < len(self.pieces):
+            self.start(now + AHEAD)
         self.ticks += 1
 
     def tick_until(self, piece):
@@ -379,7 +385,7 @@
     for full, shard in (
         (wq_full, wq_raw.shape[1]), (wp_full, wp_wide.shape[0]), (wi_full, wi_raw.shape[0]), (wo_full, wo_raw.shape[0])
     ):
-        unit = unit_rows(shard)
+        unit = unit_rows(shard, 48 if lists else FIRST_UNIT)
         lists.append(list(range(len(pieces), len(pieces) + shard // unit)))
         pieces += [(full, shard, first, unit) for first in range(0, shard, unit)]
     list_q, list_p, list_i, list_o = lists
@@ -392,13 +398,13 @@
     wq_full[own_rows_of(wq_full, wq_raw.shape[1]), :] = jnp.concatenate(
         [wq_raw[part_index] for part_index in range(3)], axis=1
     ).astype(HALF)
-    for piece in list_q[:3]:
+    for piece in list_q[:AHEAD]:
         gather.start(piece)
     wp_wide[...] = jnp.zeros_like(wp_wide)
     wp_wide[0:wp_raw.shape[0], :] = wp_raw[...]
     for raw, full in ((wp_wide, wp_full), (wi_raw, wi_full), (wo_raw, wo_full)):
         full[own_rows_of(full, raw.shape[0]), :] = raw[...].astype(HALF)
-    for piece in range(len(list_q[:3]), 3):
+    for piece in range(len(list_q[:AHEAD]), AHEAD):
         gather.start(piece)
 
     def ada_copy(group):
@@ -408,7 +414,7 @@
     cond_high, cond_low = split_two(silu(pick_rows(cond_picks(seg_cond, cond_ref.shape[0]), cond_ref[...])))
     cond_both = jnp.concatenate([cond_high, cond_low], axis=0)
     for group in range(6):
-        if group == 3:
+        if group in (2, 4):
             gather.tick()
         if group < 5:
             ada_copy(group + 1).start()
@@ -452,7 +458,9 @@
         hid_a[rows, :] = (normed * (1.0 + mm(chosen, modk[1])) + mm(chosen, modk[0])).astype(HALF)
         return carry
 
-    lax.fori_loop(0, tokens // share, hidden_block, 0)
+    lax.fori_loop(0, tokens // share // 2, hidden_block, 0)
+    gather.tick_until(list_q[-1] // 2)
+    lax.fori_loop(tokens // share // 2, tokens // share, hidden_block, 0)
     gather.tick_until(list_q[-1])
     for piece in list_q:
         gather.arrive(piece)
@@ -503,10 +511,10 @@
     wp_tight[...] = mm(proj_place[...], wp_full[...]).astype(HALF)
     part[0] = mm(joined, wp_tight[...]).astype(HALF)
     core_copy(0, part.at[0]).start()
-    gather.tick_until(list_i[0])
     joined = attend(at.share_of(False, True))
     part[1] = mm(joined, wp_tight[...]).astype(HALF)
     core_copy(1, part.at[1]).start()
+    gather.tick_until(list_i[0])
     joined = attend(at.share_of(True, False))
     summed = mm(joined, wp_tight[...])
     core_copy(0, part.at[0]).wait_recv()
@@ -537,6 +545,7 @@
     across = hid_rows(True, False)
     onward = remote(across, across, gat_send.at[2], gat_recv.at[2], at.core_peer())
     gather.tick_until(list_i[-1])
+    gather.tick_until(list_o[0])
     remote(across, across, gat_send.at[1], gat_recv.at[1], at.y_peer()).wait_recv()
     onward.start()
     for piece in list_i:
@@ -545,7 +554,6 @@
     remote(beside, beside, gat_send.at[0], gat_recv.at[0], at.core_peer()).wait_recv()
     far = hid_rows(True, True)
     remote(far, far, gat_send.at[2], gat_recv.at[2], at.core_peer()).wait_recv()
-    gather.tick_until(list_o[0])
 
     def inner_block(index, carry):
         rows = rows_at(index * share, share)
@@ -673,7 +681,7 @@
     shards = (sizes["shard"], pad_rows, sizes["shard"], hidden // dp_count)
     xs = line_length(dp_count)
     zs = dp_count // xs
-    units = sum(shard // unit_rows(shard) for shard in shards)
+    units = shards[0] // unit_rows(shards[0], FIRST_UNIT) + sum(shard // unit_rows(shard) for shard in shards[1:])
     place = jnp.asarray(placing(columns, own_rows, pad_rows, dp_count), HALF)
     shapes = [
         ((width, 3 * columns), HALF), ((columns, width), HALF), ((width, hidden), HALF),
@@ -875,7 +883,7 @@
         (whole_o, xin_o, zin_o), (whole_i, xin_i, zin_i), (whole_p, xin_p, zin_p), (whole_q, xin_q, zin_q)
     ):
         shard = x_in.shape[2]
-        unit = unit_rows(shard)
+        unit = unit_rows(shard, LAST_UNIT if whole is whole_q else 48)
         pieces.append([(whole, x_in, z_in, shard, first, unit) for first in range(0, shard, unit)])
     flat = [piece for group in pieces for piece in group]
     scatter = Scatter(at, flat, (x_send, x_recv), (z_send, z_recv))
@@ -1075,21 +1083,23 @@
     loads["wp"].wait()
     loads["heads"].wait()
     loads["lse"].wait()
+    for piece in list_o[2:]:
+        scatter.pass_on(piece)
     grad_a_sum = grad_att(at.share_of(False, False))
     attend_back(at.share_of(False, False))
-    for piece in list_o[2:]:
-        scatter.pass_on(piece)
     remote(beside, beside, gat_send.at[0], gat_recv.at[0], at.core_peer()).wait_recv()
     grad_a_sum = grad_a_sum + grad_att(at.share_of(False, True))
     remote(across, across, gat_send.at[1], gat_recv.at[1], at.y_peer()).wait_recv()
     onward.start()
     attend_back(at.share_of(False, True))
     grad_a_sum = grad_a_sum + grad_att(at.share_of(True, False))
+    scatter.pass_on(list_i[0])
     attend_back(at.share_of(True, False))
-    scatter.pass_on(list_i[0])
     remote(far, far, gat_send.at[2], gat_recv.at[2], at.core_peer()).wait_recv()
     grad_a_sum = grad_a_sum + grad_att(at.share_of(True, True))
     attend_back(at.share_of(True, True))
+    for piece in list_i[1:2]:
+        scatter.pass_on(piece)
     packs[at.dp, 2:3, 0:width] = grad_a_sum
     loads["att"].wait()
     proj_grad = mm_tn(att[...], grad_a[...]).astype(HALF)
@@ -1110,7 +1120,7 @@
         return total + jnp.sum(values, axis=0, keepdims=True)
 
     packs[at.dp, 0:1, 0:3 * columns] = lax.fori_loop(0, blocks, join_block, jnp.zeros((1, 3 * columns), FLOAT))
-    for piece in list_i[1:2]:
+    for piece in list_i[2:]:
         scatter.pass_on(piece)
     loads["hid_a"].wait()
 
@@ -1131,7 +1141,7 @@
         saves.append(copy)
 
     def mod_sums():
-        for piece in list_i[2:] + list_p:
+        for piece in list_p:
             scatter.pass_on(piece)
         ff_copy.wait_recv()
         branch_b = ff_own[...] + ff_in[...].astype(FLOAT) + shared_bias[1:2, :]
@@ -1141,7 +1151,7 @@
         mod_start(0)
         for part_index in (2, 3):
             spread.start(part_index)
-        for piece in list_q[:1]:
+        for piece in list_q[:len(list_q) // 3]:
             scatter.pass_on(piece)
 
     unit = lax.broadcasted_iota(jnp.int32, (segs, 1), 0) == lax.broadcasted_iota(jnp.int32, (1, segs), 1)
@@ -1161,7 +1171,7 @@
     keep_mod(0, grad_hid_a)
     keep_mod(1, grad_hid_a * normed)
     mod_start(1)
-    for piece in list_q[1:]:
+    for piece in list_q[len(list_q) // 3:]:
         scatter.pass_on(piece)
     for part_index in (2, 3, 0):
         spread.pass_on(part_index)
@@ -1201,7 +1211,7 @@
     zs = dp_count // xs
     shards = (hidden // dp_count, width // dp_count, pad_rows, width // dp_count)
     wholes = ((hidden, width), (width, hidden), (dp_count * pad_rows, width), (width, 3 * columns))
-    units = sum(shard // unit_rows(shard) for shard in shards)
+    units = sum(shard // unit_rows(shard) for shard in shards[:3]) + shards[3] // unit_rows(shards[3], LAST_UNIT)
     place = jnp.asarray(placing(columns, own_rows, pad_rows, dp_count).T, HALF)
     pack_width = max(width, hidden, 3 * columns)
     shapes = [((share, width), HALF), ((share, width), FLOAT)]

time: 289 us -> 285 us (0.986)
  Pallas kernels: 281 us -> 277 us
    pallas_call x1, Pallas kernels: 119 us -> 114 us  [run_forward(): pl.pallas_call(functools.partial(forward_kernel, sizes), out_shape=[jax.S...]
where the time goes in v1:
time: 285 us; the launch traced here: 282 us
  Pallas kernels  277 us (97%)
  local copies, waits for them, and re-layouts  4.21 us (1%)
    pallas_call x1, Pallas kernels, run_backward(): pl.pallas_call(functools.partial(backward_kernel, sizes), out_shape=[jax....  130 us
    pallas_call x1, Pallas kernels, run_forward(): pl.pallas_call(functools.partial(forward_kernel, sizes), out_shape=[jax.S...  114 us
    pallas_call x1, Pallas kernels, run_update(): pl.pallas_call(functools.partial(update_kernel, sizes), out_shape=outs, i...  24.6 us
    pallas_call x1, Pallas kernels, run_cond(): pl.pallas_call(functools.partial(cond_kernel, sizes), out_shape=jax.Shape...  8.86 us

profile of v1, /device:TPU:0, one launch (start us, length us, event | category | flops | bytes accessed | tf_op | source)
XLA Modules:
  0.0 282.2 jit_solution(14499372741212876325)
XLA Ops:
  0.7 1.7 copy.63.seg_col
  2.4 113.9 %forward.1 = (bf16[1152,864]{1,0:T(8,128)(2,1)}, bf16[288,1152]{1,0:T(8,128)(2,1)}, bf16[1152,1152]{1,0:T(8,128)(2,1)}, bf16[1152,1152]{1,0:T(8,128)(2,1)}, bf16...) custom-call(bf16[1024,1152]{1,0:T(8,128)(2,1)} %x_in.1, ...), custom_call_target="tpu_custom_call" | custom-call | tf_op jit(solution)/shard_map/forward/pallas_call | solution.py:712
  116.2 129.7 %backward.1 = (bf16[256,1152]{1,0:T(8,128)(2,1)}, f32[256,1152]{1,0:T(8,128)}, bf16[4,144,864]{2,1,0:T(8,128)(2,1)}, bf16[4,48,1152]{2,1,0:T(8,128)(2,1)}, bf16[...) custom-call(s32[1024,1]{1,0:T(8,128)} %copy.63.seg_col, ...), custom_call_target="tpu_custom_call" | custom-call | tf_op jit(solution)/shard_map/backward/pallas_call | solution.py:1245
  246.0 0.0 copy-start.2
  246.0 24.6 %update.1 = (f32[32,1152]{1,0:T(8,128)}, f32[9,288]{1,0:T(8,128)}, f32[9,288]{1,0:T(8,128)}, f32[9,288]{1,0:T(8,128)}, f32[1152]{0:T(1024)}, /*index=5*/f32[1152...) custom-call(f32[32,1152]{1,0:T(8,128)} %cond_ref.5, ...), custom_call_target="tpu_custom_call" | custom-call | tf_op jit(solution)/shard_map/update/pallas_call | solution.py:1611
  270.6 0.0 copy-start
  270.6 8.9 %cond.1 = f32[32,1152]{1,0:T(8,128)} custom-call(f32[32,1152]{1,0:T(8,128)} %cond_ref.5, f32[32,1152]{1,0:T(8,128)} %get-tuple-element.110.part_in), custom_call_target="tpu_custom_call" | custom-call | tf_op jit(solution)/shard_map/cond/pallas_call | solution.py:1665
  279.5 0.0 copy-start.1
  279.5 0.0 copy-done.2
  279.5 0.8 copy.67
  280.3 0.0 copy-done
  280.3 1.0 copy.68
  281.3 0.0 copy-done.1
  281.3 0.7 copy.69
Async XLA Ops:
  246.0 33.5 %copy-start.2 = (bf16[256,1152]{1,0:T(8,128)(2,1)S(1)}, bf16[256,1152]{1,0:T(8,128)(2,1)}, u32[]{:S(2)}) copy-start(bf16[256,1152]{1,0:T(8,128)(2,1)} %get-tuple-element.170) | copy-start | bytes 1769476
  270.6 9.7 %copy-start = (f32[256,1152]{1,0:T(8,128)S(1)}, f32[256,1152]{1,0:T(8,128)}, u32[]{:S(2)}) copy-start(f32[256,1152]{1,0:T(8,128)} %get-tuple-element.171) | copy-start | bytes 3538948
  279.5 1.9 copy-start.1

commit v2 on v1

--- a/solution.py
+++ b/solution.py
@@ -242,7 +242,7 @@
     return pl.ds(pl.multiple_of(start, 16), count)
 
 
-AHEAD = 3
+AHEAD = 2
 
 
 def unit_rows(shard, most=48):
@@ -321,7 +321,7 @@
 
     def tick(self):
         now = self.ticks
-        for away in range(1, self.hops + 1):
+        for away in range(self.hops, 0, -1):
             if 0 <= now - away + 1 < len(self.pieces):
                 self.pass_on(now - away + 1, away)
         if now + AHEAD < len(self.pieces):

time: 285 us -> 277 us (0.972)
  Pallas kernels: 277 us -> 269 us
    pallas_call x1, Pallas kernels: 114 us -> 106 us  [run_forward(): pl.pallas_call(functools.partial(forward_kernel, sizes), out_shape=[jax.S...]
where the time goes in v2:
time: 277 us; the launch traced here: 274 us
  Pallas kernels  269 us (97%)
  local copies, waits for them, and re-layouts  4.21 us (2%)
    pallas_call x1, Pallas kernels, run_backward(): pl.pallas_call(functools.partial(backward_kernel, sizes), out_shape=[jax....  129 us
    pallas_call x1, Pallas kernels, run_forward(): pl.pallas_call(functools.partial(forward_kernel, sizes), out_shape=[jax.S...  106 us
    pallas_call x1, Pallas kernels, run_update(): pl.pallas_call(functools.partial(update_kernel, sizes), out_shape=outs, i...  24.6 us
    pallas_call x1, Pallas kernels, run_cond(): pl.pallas_call(functools.partial(cond_kernel, sizes), out_shape=jax.Shape...  9.49 us

profile of v2, /device:TPU:0, one launch (start us, length us, event | category | flops | bytes accessed | tf_op | source)
XLA Modules:
  0.0 274.0 jit_solution(14745707512410869670)
XLA Ops:
  0.7 1.7 copy.63.seg_col
  2.4 106.1 %forward.1 = (bf16[1152,864]{1,0:T(8,128)(2,1)}, bf16[288,1152]{1,0:T(8,128)(2,1)}, bf16[1152,1152]{1,0:T(8,128)(2,1)}, bf16[1152,1152]{1,0:T(8,128)(2,1)}, bf16...) custom-call(bf16[1024,1152]{1,0:T(8,128)(2,1)} %x_in.1, ...), custom_call_target="tpu_custom_call" | custom-call | tf_op jit(solution)/shard_map/forward/pallas_call | solution.py:712
  108.5 128.6 %backward.1 = (bf16[256,1152]{1,0:T(8,128)(2,1)}, f32[256,1152]{1,0:T(8,128)}, bf16[4,144,864]{2,1,0:T(8,128)(2,1)}, bf16[4,48,1152]{2,1,0:T(8,128)(2,1)}, bf16[...) custom-call(s32[1024,1]{1,0:T(8,128)} %copy.63.seg_col, ...), custom_call_target="tpu_custom_call" | custom-call | tf_op jit(solution)/shard_map/backward/pallas_call | solution.py:1245
  237.1 0.0 copy-start.2
  237.1 24.6 %update.1 = (f32[32,1152]{1,0:T(8,128)}, f32[9,288]{1,0:T(8,128)}, f32[9,288]{1,0:T(8,128)}, f32[9,288]{1,0:T(8,128)}, f32[1152]{0:T(1024)}, /*index=5*/f32[1152...) custom-call(f32[32,1152]{1,0:T(8,128)} %cond_ref.5, ...), custom_call_target="tpu_custom_call" | custom-call | tf_op jit(solution)/shard_map/update/pallas_call | solution.py:1611
  261.8 0.0 copy-start
  261.8 9.5 %cond.1 = f32[32,1152]{1,0:T(8,128)} custom-call(f32[32,1152]{1,0:T(8,128)} %cond_ref.5, f32[32,1152]{1,0:T(8,128)} %get-tuple-element.110.part_in), custom_call_target="tpu_custom_call" | custom-call | tf_op jit(solution)/shard_map/cond/pallas_call | solution.py:1665
  271.3 0.0 copy-start.1
  271.3 0.0 copy-done.2
  271.3 0.8 copy.67
  272.1 0.0 copy-done
  272.1 1.0 copy.68
  273.1 0.0 copy-done.1
  273.1 0.7 copy.69
Async XLA Ops:
  237.1 34.2 %copy-start.2 = (bf16[256,1152]{1,0:T(8,128)(2,1)S(1)}, bf16[256,1152]{1,0:T(8,128)(2,1)}, u32[]{:S(2)}) copy-start(bf16[256,1152]{1,0:T(8,128)(2,1)} %get-tuple-element.170) | copy-start | bytes 1769476
  261.8 10.3 %copy-start = (f32[256,1152]{1,0:T(8,128)S(1)}, f32[256,1152]{1,0:T(8,128)}, u32[]{:S(2)}) copy-start(f32[256,1152]{1,0:T(8,128)} %get-tuple-element.171) | copy-start | bytes 3538948
  271.3 1.9 copy-start.1
